TPU v7x, 128 devices: a whole 4x4x4 slice. The times are simulated.
128 devices in a mesh: seq: 16 (over z, y), trk: 8 (over x, core).
Axes of the slice: x: 4, y: 4, z: 4, core: 2. Of those that a mesh axis runs over, the one named last changes fastest.
Arguments:
- inputs: bfloat16 [8, 4096, 1536], P('trk', 'seq'), may hold values from -6 to 6
- layernorm_gain: float32 [1536], replicated, may hold values from 0.5 to 1.5
- dilated_weight: bfloat16 [3, 1536, 768], replicated, may hold values from -0.09375 to 0.09375
- mix_weight: bfloat16 [768, 1536], replicated, may hold values from -0.21875 to 0.21875
- head_weight: bfloat16 [1536, 4096], P(None, 'trk'), may hold values from -0.15625 to 0.15625
- head_bias: float32 [4096], P('trk'), may hold values from -1 to 1
- stored_tiles: bfloat16 [512, 4096, 128], P(('seq', 'trk')), may hold values from 0 to 4
- slot_tiles: int32 [512], replicated, may hold values from -1 to 255, as said below
Outputs:
- input_grad: float32 [8, 4096, 1536], P('trk', 'seq')
Inputs may be any that keep to these rules, and one draw needn't show every extreme that they name: `slot_tiles`: slots are listed device by device in mesh order, 4 for each device. Each tile number s * 32 + k (sequence s, track block k) stands in exactly one slot; the others hold -1. Track block k belongs to group k // 4. The devices of one trk index hold together at most 8 tiles of each group, and each group has exactly 8 tiles at some trk index. Some device's slots are all used.
All inputs are finite; a program needn't handle non-finite values.
Results may differ from a plain program's by a relative error of at most 0.011.
Values may be sent and summed in bfloat16 or wider, within the bound.
No kernel may reach another device: no remote copies, remote signals or barrier semaphores. Data moves between devices by JAX's collectives and lax.ppermute only.
A program may use at most 128 MiB of HBM per device.

v0:
```python
import jax
import jax.numpy as jnp
from jax import lax
from jax.sharding import PartitionSpec as P

DILATION_STEP = 64


SQRT_HALF = 0.7071067811865476
INV_SQRT_TAU = 0.3989422804014327


def with_halo(value, sides, width):
    for axis, dim in sides:
        size, length = (lax.axis_size(axis), value.shape[dim])
        up = [(i, (i + 1) % size) for i in range(size - 1)]
        down = [(j, i) for i, j in up]
        last = lax.slice_in_dim(value, length - width, length, axis=dim)
        initial = lax.slice_in_dim(value, 0, width, axis=dim)
        before = lax.ppermute(last, axis, up)
        after = lax.ppermute(initial, axis, down)
        value = jnp.concatenate([before, value, after], axis=dim)
    return value


def gelu_exact(v):
    return 0.5 * v * (1.0 + lax.erf(v * SQRT_HALF))


def gelu_slope(v):
    return 0.5 * (1.0 + lax.erf(v * SQRT_HALF)) + v * jnp.exp(-0.5 * v * v) * INV_SQRT_TAU


def shards(
    inputs,
    layernorm_gain,
    dilated_weight,
    mix_weight,
    head_weight,
    head_bias,
    stored_tiles,
    slot_tiles,
):
    n_seq = lax.axis_size("seq")
    n_trk = lax.axis_size("trk")
    trk_index = lax.axis_index("trk")
    bins = inputs.shape[1]
    width = inputs.shape[2]
    dilation_spacing = DILATION_STEP
    own_tracks = head_weight.shape[1]
    tile_width = stored_tiles.shape[2]
    own_spans = own_tracks // tile_width
    slots = stored_tiles.shape[0]
    blocks = own_spans * n_trk
    limit = 2 * blocks // n_trk
    n_tiles = n_trk * blocks
    depth = n_seq * slots
    pieces = lax.all_to_all(stored_tiles, "seq", split_axis=1, concat_axis=0, tiled=True)
    table = slot_tiles.reshape(n_seq, n_trk, slots).transpose(1, 0, 2).reshape(n_trk, depth)
    valid = table >= 0
    groups = jnp.arange(n_trk, dtype=jnp.int32)
    owner = jnp.where(valid, table % blocks // own_spans, n_trk)
    marks = (owner[:, :, None] == groups[None, None, :]).astype(jnp.int32)
    before = jnp.cumsum(marks, axis=1) - marks
    rank = jnp.sum(before * marks, axis=2)
    target_slot = jnp.where(valid, owner * limit + rank, n_trk * limit)
    mine = lax.dynamic_index_in_dim(target_slot, trk_index, 0, keepdims=False)
    source = (
        jnp.full((n_trk * limit,), depth, jnp.int32)
        .at[mine]
        .set(jnp.arange(depth, dtype=jnp.int32), mode="drop")
    )
    outgoing = jnp.take(pieces, source, axis=0, mode="fill", fill_value=0)
    arrived = lax.all_to_all(outgoing, "trk", split_axis=0, concat_axis=0, tiled=True)
    arrival = groups[:, None] * limit + rank
    safe = jnp.where(valid, table, n_tiles)
    lookup = jnp.zeros((n_tiles,), jnp.int32).at[safe].set(arrival, mode="drop")
    wanted = (
        groups[:, None] * blocks
        + trk_index * own_spans
        + jnp.arange(own_spans, dtype=jnp.int32)[None, :]
    )
    found = jnp.take(lookup, wanted.reshape(-1))
    target = jnp.take(arrived, found, axis=0).reshape(n_trk, own_spans, bins, tile_width)
    target = target.transpose(0, 2, 1, 3).reshape(n_trk * bins, own_tracks)
    x_rows = inputs[0].astype(jnp.float32)
    centre_offset = x_rows - jnp.mean(x_rows, axis=1, keepdims=True)
    inverse_deviation = lax.rsqrt(
        jnp.mean(centre_offset * centre_offset, axis=1, keepdims=True) + 1e-05
    )
    centred_normalized = centre_offset * inverse_deviation
    normalized_rows = centred_normalized * layernorm_gain
    activated_rows = gelu_exact(normalized_rows).astype(jnp.bfloat16)
    padded_input = with_halo(activated_rows, (("seq", 0),), dilation_spacing)
    preactivation = jnp.zeros((bins, dilated_weight.shape[2]), jnp.float32)
    for tap_number in range(3):
        preactivation = preactivation + jnp.dot(
            padded_input[tap_number * dilation_spacing : tap_number * dilation_spacing + bins],
            dilated_weight[tap_number],
            preferred_element_type=jnp.float32,
        )
    inner = gelu_exact(preactivation).astype(jnp.bfloat16)
    embed = (x_rows + jnp.dot(inner, mix_weight, preferred_element_type=jnp.float32)).astype(
        jnp.bfloat16
    )
    rows = lax.all_gather(embed[None], "trk", axis=0, tiled=True)
    logits = (
        jnp.dot(rows.reshape(n_trk * bins, width), head_weight, preferred_element_type=jnp.float32)
        + head_bias
    )
    pred = jax.nn.softplus(logits)
    d_logits = ((1.0 - target.astype(jnp.float32) / pred) * jax.nn.sigmoid(logits)).astype(
        jnp.bfloat16
    )
    local_grads = lax.all_to_all(
        d_logits.reshape(n_trk, bins, own_tracks), "trk", split_axis=0, concat_axis=2, tiled=True
    )
    full_head = lax.all_gather(head_weight, "trk", axis=1, tiled=True)
    partial_pieces = jnp.einsum(
        "qnp,enp->nqe",
        local_grads.reshape(bins, n_trk, own_tracks),
        full_head.reshape(width, n_trk, own_tracks),
        preferred_element_type=jnp.float32,
    ).astype(jnp.bfloat16)
    d_embed = jnp.sum(partial_pieces, axis=0, dtype=jnp.float32)
    d_half = d_embed.astype(jnp.bfloat16)
    d_inner = lax.dot_general(
        d_half, mix_weight, (((1,), (1,)), ((), ())), preferred_element_type=jnp.float32
    )
    preact_gradient = (d_inner * gelu_slope(preactivation)).astype(jnp.bfloat16)
    padded_gradient = with_halo(preact_gradient, (("seq", 0),), dilation_spacing)
    d_act = jnp.zeros((bins, width), jnp.float32)
    for tap_number in range(3):
        start_offset = (2 - tap_number) * dilation_spacing
        d_act = d_act + lax.dot_general(
            padded_gradient[start_offset : start_offset + bins],
            dilated_weight[tap_number],
            (((1,), (1,)), ((), ())),
            preferred_element_type=jnp.float32,
        )
    scaled_rows = d_act * gelu_slope(normalized_rows) * layernorm_gain
    backward_fn = (
        scaled_rows
        - jnp.mean(scaled_rows, axis=1, keepdims=True)
        - centred_normalized * jnp.mean(scaled_rows * centred_normalized, axis=1, keepdims=True)
    )
    return (d_embed + inverse_deviation * backward_fn)[None]


def solution(mesh):
    in_specs = (
        P("trk", "seq", None),
        P(),
        P(),
        P(),
        P(None, "trk"),
        P("trk"),
        P(("seq", "trk"), None, None),
        P(),
    )
    out_specs = P("trk", "seq", None)
    return jax.shard_map(shards, mesh=mesh, in_specs=in_specs, out_specs=out_specs, check_vma=False)
```

profile of v0, /device:TPU:56, one launch (start us, length us, event | category | flops | bytes accessed | tf_op | source)
XLA Modules:
  0.0 270.4 jit_solution(8537747377824331142)
XLA Ops:
  10.2 2.7 collective-permute-start.1
  12.8 5.6 %collective-permute-start = (bf16[64,1536]{1,0:T(8,128)(2,1)S(1)}, bf16[64,1536]{1,0:T(8,128)(2,1)S(1)}, u32[]{:S(2)}, u32[]{:S(2)}) collective-permute-start(bf16[64,1536]{1,0:T(8,128)(2,1)S(1)} %get-tuple-element.7), channel_id=1, source_target_pairs={{0,8},{8,16},{16,24},{24,32},{32,40},{40,48},{48,56},{56,64},{64,7... | collective-permute-start | bytes 589832 | tf_op jit(solution)/shard_map/ppermute | solution.py:20
  18.4 2.8 %fusion.14 = f32[256,768]{1,0:T(8,128)S(1)} fusion(bf16[3,1536,768]{2,1,0:T(8,128)(2,1)} %param.10, bf16[1,256,1536]{2,1,0:T(8,128)(2,1)S(1)} %copy-done.1, f32[1536]{0:T(1024)S(1)} %copy-done.2, f32[256]{0:T(256)S(1)} %add_rsqrt_fusion, f32[256]{0:T(256)S(1)} %broadcast_multiply_fusion.2), kind=kOutput, calls=%fused_computation.29 | convolution fusion | flops 607518720 | bytes 3940352 | tf_op jit(solution)/shard_map/dot_general | solution.py:97
  25.7 2.6 copy.55
  28.3 7.6 %copy.51 = bf16[4,4096,128]{2,0,1:T(4,128)(2,1)} copy(bf16[4,4096,128]{2,1,0:T(8,128)(2,1)} %param.14) | data formatting | bytes 8388608 | tf_op args[6]
  35.9 8.6 %all-to-all-start = ((bf16[4,4096,128]{2,0,1:T(4,128)(2,1)}), bf16[4,4096,128]{2,0,1:T(4,128)(2,1)}, u32[]{:S(2)}, u32[]{:S(2)}) async-start(bf16[4,4096,128]{2,0,1:T(4,128)(2,1)} %copy.51), calls=%async_computation | async-start | bytes 8388608 | tf_op jit(solution)/shard_map/all_to_all | solution.py:58
  47.2 52.4 %all-to-all-done = bf16[4,4096,128]{2,0,1:T(4,128)(2,1)} async-done(((bf16[4,4096,128]{2,0,1:T(4,128)(2,1)}), bf16[4,4096,128]{2,0,1:T(4,128)(2,1)}, u32[]{:S(2)}, u32[]{:S(2)}) %all-to-all-start) | async-done | bytes 4194336 | tf_op jit(solution)/shard_map/all_to_all | solution.py:58
  99.6 2.8 %copy.52 = bf16[4,4096,128]{2,1,0:T(8,128)(2,1)S(1)} copy(bf16[4,4096,128]{2,0,1:T(4,128)(2,1)} %all-to-all-done) | data formatting | bytes 8388608 | tf_op jit(solution)/shard_map/all_to_all | solution.py:58
  104.7 5.3 %gather_fusion.1 = bf16[64,256,128]{2,1,0:T(8,128)(2,1)} fusion(bf16[64,256,128]{2,1,0:T(8,128)(2,1)} %bitcast.129, s32[1024]{0:T(1024)S(1)} %pad_clamp_fusion.1), kind=kCustom, calls=%fused_computation.1 | custom fusion | bytes 8388864 | tf_op jit(solution)/shard_map/jit(_take)/gather | solution.py:73
  110.0 4.6 %broadcast_select_fusion = bf16[64,256,128]{2,1,0:T(8,128)(2,1)} fusion(bf16[64,256,128]{2,1,0:T(8,128)(2,1)} %gather_fusion.1, pred[64]{0:T(512)(128)(4,1)S(1)} %compare_and_fusion.1), kind=kLoop, calls=%fused_computation.11 | loop fusion | flops 2097152 | bytes 8388672 | tf_op jit(solution)/shard_map/jit(_take)/select_n | solution.py:73
  114.6 4.6 %all-to-all-start.1 = ((bf16[64,256,128]{2,1,0:T(8,128)(2,1)}), bf16[64,256,128]{2,1,0:T(8,128)(2,1)}, u32[]{:S(2)}, u32[]{:S(2)}) async-start(bf16[64,256,128]{2,1,0:T(8,128)(2,1)} %broadcast_select_fusion), calls=%async_computation.1 | async-start | bytes 8388608 | tf_op jit(solution)/shard_map/all_to_all | solution.py:74
  119.7 2.6 scatter_custom_fusion
  123.2 58.3 %all-to-all-done.1 = bf16[64,256,128]{2,1,0:T(8,128)(2,1)} async-done(((bf16[64,256,128]{2,1,0:T(8,128)(2,1)}), bf16[64,256,128]{2,1,0:T(8,128)(2,1)}, u32[]{:S(2)}, u32[]{:S(2)}) %all-to-all-start.1) | async-done | bytes 4194336 | tf_op jit(solution)/shard_map/all_to_all | solution.py:74
  181.5 4.3 %gather_fusion.2 = bf16[32,256,128]{2,1,0:T(8,128)(2,1)} fusion(bf16[64,256,128]{2,1,0:T(8,128)(2,1)} %all-to-all-done.1, s32[1024]{0:T(1024)S(1)} %pad_clamp_fusion), kind=kCustom, calls=%fused_computation.2 | custom fusion | bytes 4194432 | tf_op jit(solution)/shard_map/jit(_take)/gather | solution.py:84
  187.8 4.7 %copy.54 = f32[8,256,4,128]{3,2,1,0:T(4,128)} copy(f32[8,256,4,128]{3,1,2,0:T(8,128)S(1)} %convert_bitcast_fusion) | data formatting | bytes 8388608 | tf_op jit(solution)/shard_map/convert_element_type | solution.py:112
  192.5 11.0 %fusion.3 = bf16[2048,512]{1,0:T(8,128)(2,1)S(1)} fusion(f32[256,8,4,128]{3,2,1,0:T(4,128)} %bitcast.132, bf16[2048,1536]{1,0:T(8,128)(2,1)} %all-gather.6.cloned.1.call-done, bf16[1536,512]{1,0:T(8,128)(2,1)} %param.12, f32[512]{0:T(512)S(1)} %copy-done.5), kind=kOutput, calls=%fused_computation.12 | convolution fusion | flops 3235905536 | bytes 14157824 | tf_op jit(solution)/shard_map/dot_general | solution.py:108
  203.5 30.8 %all_to_all.38 = bf16[8,256,512]{2,1,0:T(8,128)(2,1)} all-to-all(bf16[8,256,512]{2,1,0:T(8,128)(2,1)S(1)} %bitcast.133), channel_id=1, replica_groups=mesh['seq'=16,'trk'=8] {'trk'}, dimensions={0} | all-to-all | bytes 4194304 | tf_op jit(solution)/shard_map/all_to_all | solution.py:115
  234.3 8.8 %convert_reduce_fusion = f32[256,1536]{1,0:T(8,128)S(1)} fusion(bf16[1536,8,512]{0,2,1:T(8,128)(2,1)} %bitcast.138, bf16[8,256,512]{2,1,0:T(8,128)(2,1)} %all_to_all.38), kind=kOutput, calls=%fused_computation.5 | convolution fusion | flops 3230269440 | bytes 16252928 | tf_op jit(solution)/shard_map/qnp,enp->nqe/dot_general | solution.py:119
  244.0 3.4 %collective-permute-start.3 = (bf16[64,768]{1,0:T(8,128)(2,1)S(1)}, bf16[64,768]{1,0:T(8,128)(2,1)S(1)}, u32[]{:S(2)}, u32[]{:S(2)}) collective-permute-start(bf16[64,768]{1,0:T(8,128)(2,1)S(1)} %get-tuple-element.10), channel_id=1, source_target_pairs={{0,8},{8,16},{16,24},{24,32},{32,40},{40,48},{48,56},{56,64},{64,7... | collective-permute-start | bytes 294920 | tf_op jit(solution)/shard_map/ppermute | solution.py:20
  247.4 2.5 fusion.12
  249.9 2.4 collective-permute-start.2
  252.4 2.5 fusion.8
  254.9 3.7 %collective-permute-done.2 = bf16[64,768]{1,0:T(8,128)(2,1)S(1)} collective-permute-done((bf16[64,768]{1,0:T(8,128)(2,1)S(1)}, bf16[64,768]{1,0:T(8,128)(2,1)S(1)}, u32[]{:S(2)}, u32[]{:S(2)}) %collective-permute-start.2) | collective-permute-done | bytes 98336 | tf_op jit(solution)/shard_map/ppermute | solution.py:21
  258.5 3.4 %fusion.105 = (f32[256]{0:T(256)S(1)}, f32[256]{0:T(256)S(1)}, f32[256,1536]{1,0:T(8,128)S(1)}) fusion(f32[256]{0:T(256)S(1)} %add_rsqrt_fusion, f32[256]{0:T(256)S(1)} %broadcast_multiply_fusion.2, bf16[1,256,1536]{2,1,0:T(8,128)(2,1)S(1)} %copy-done.1, f32[1536]{0:T(1024)S(1)} %copy-done.2, f32[256,1536]{1,0:T(8,128)S(1)} %fusion.8, ...), kind=kOutput, calls=%fused_computation.158 | convolution fusion | flops 612236800 | bytes 8366080 | tf_op jit(solution)/shard_map/dot_general | solution.py:135
  (69 shorter events, 19.0 us)
Async XLA Ops:
  6.5 17.4 %copy-start = (bf16[768,1536]{1,0:T(8,128)(2,1)S(1)}, bf16[768,1536]{1,0:T(8,128)(2,1)}, u32[]{:S(2)}) copy-start(bf16[768,1536]{1,0:T(8,128)(2,1)} %param.11) | copy-start | bytes 7077892
  6.5 3.0 %copy-start.1 = (bf16[1,256,1536]{2,1,0:T(8,128)(2,1)S(1)}, bf16[1,256,1536]{2,1,0:T(8,128)(2,1)}, u32[]{:S(2)}) copy-start(bf16[1,256,1536]{2,1,0:T(8,128)(2,1)} %param.8) | copy-start | bytes 2359300
  6.5 3.0 %copy-start.2 = (f32[1536]{0:T(1024)S(1)}, f32[1536]{0:T(1024)}, u32[]{:S(2)}) copy-start(f32[1536]{0:T(1024)} %param.9) | copy-start | bytes 18436
  6.5 186.0 %all-gather.6.cloned.1.call-start = ((), (), s32[]{:S(2)}) async-start(), calls=%async_computation.4 | async-start | bytes 7077888 | tf_op jit(solution)/shard_map/all_gather | solution.py:106
  10.2 11.0 %collective-permute-start.1 = (bf16[64,1536]{1,0:T(8,128)(2,1)S(1)}, bf16[64,1536]{1,0:T(8,128)(2,1)S(1)}, u32[]{:S(2)}, u32[]{:S(2)}) collective-permute-start(bf16[64,1536]{1,0:T(8,128)(2,1)S(1)} %get-tuple-element.8), channel_id=1, source_target_pairs={{8,0},{16,8},{24,16},{32,24},{40,32},{48,40},{56,48},{64,56},{72,6... | collective-permute-start | bytes 589832 | tf_op jit(solution)/shard_map/ppermute | solution.py:21
  12.8 8.4 %copy-start.4 = (bf16[3,1536,768]{2,1,0:T(8,128)(2,1)S(1)}, bf16[3,1536,768]{2,1,0:T(8,128)(2,1)}, u32[]{:S(2)}) copy-start(bf16[3,1536,768]{2,1,0:T(8,128)(2,1)} %param.10) | copy-start | bytes 21233668
  12.8 9.4 %collective-permute-start = (bf16[64,1536]{1,0:T(8,128)(2,1)S(1)}, bf16[64,1536]{1,0:T(8,128)(2,1)S(1)}, u32[]{:S(2)}, u32[]{:S(2)}) collective-permute-start(bf16[64,1536]{1,0:T(8,128)(2,1)S(1)} %get-tuple-element.7), channel_id=1, source_target_pairs={{0,8},{8,16},{16,24},{24,32},{32,40},{40,48},{48,56},{56,64},{64,7... | collective-permute-start | bytes 589832 | tf_op jit(solution)/shard_map/ppermute | solution.py:20
  23.1 0.9 copy-start.6
  25.6 208.7 %all-gather.4.cloned.1.call-start = ((), (), s32[]{:S(2)}) async-start(), calls=%async_computation.3 | async-start | bytes 14155776 | tf_op jit(solution)/shard_map/all_gather | solution.py:118
  35.9 8.6 %copy-start.3 = (s32[512]{0:T(512)S(1)}, s32[512]{0:T(512)}, u32[]{:S(2)}) copy-start(s32[512]{0:T(512)} %param.15) | copy-start | bytes 6148
  35.9 63.7 %all-to-all-start = ((bf16[4,4096,128]{2,0,1:T(4,128)(2,1)}), bf16[4,4096,128]{2,0,1:T(4,128)(2,1)}, u32[]{:S(2)}, u32[]{:S(2)}) async-start(bf16[4,4096,128]{2,0,1:T(4,128)(2,1)} %copy.51), calls=%async_computation | async-start | bytes 8388608 | tf_op jit(solution)/shard_map/all_to_all | solution.py:58
  114.6 66.9 %all-to-all-start.1 = ((bf16[64,256,128]{2,1,0:T(8,128)(2,1)}), bf16[64,256,128]{2,1,0:T(8,128)(2,1)}, u32[]{:S(2)}, u32[]{:S(2)}) async-start(bf16[64,256,128]{2,1,0:T(8,128)(2,1)} %broadcast_select_fusion), calls=%async_computation.1 | async-start | bytes 8388608 | tf_op jit(solution)/shard_map/all_to_all | solution.py:74
  187.8 4.7 %copy-start.5 = (f32[512]{0:T(512)S(1)}, f32[512]{0:T(512)}, u32[]{:S(2)}) copy-start(f32[512]{0:T(512)} %param.13) | copy-start | bytes 6148
  234.3 8.8 %copy-start.7 = (f32[256,768]{1,0:T(8,128)S(1)}, f32[256,768]{1,0:T(8,128)}, u32[]{:S(2)}) copy-start(f32[256,768]{1,0:T(8,128)} %copy-done.6) | copy-start | bytes 2359300
  244.0 8.3 %collective-permute-start.3 = (bf16[64,768]{1,0:T(8,128)(2,1)S(1)}, bf16[64,768]{1,0:T(8,128)(2,1)S(1)}, u32[]{:S(2)}, u32[]{:S(2)}) collective-permute-start(bf16[64,768]{1,0:T(8,128)(2,1)S(1)} %get-tuple-element.10), channel_id=1, source_target_pairs={{0,8},{8,16},{16,24},{24,32},{32,40},{40,48},{48,56},{56,64},{64,7... | collective-permute-start | bytes 294920 | tf_op jit(solution)/shard_map/ppermute | solution.py:20
  249.9 8.6 %collective-permute-start.2 = (bf16[64,768]{1,0:T(8,128)(2,1)S(1)}, bf16[64,768]{1,0:T(8,128)(2,1)S(1)}, u32[]{:S(2)}, u32[]{:S(2)}) collective-permute-start(bf16[64,768]{1,0:T(8,128)(2,1)S(1)} %get-tuple-element.9), channel_id=1, source_target_pairs={{8,0},{16,8},{24,16},{32,24},{40,32},{48,40},{56,48},{64,56},{72,6... | collective-permute-start | bytes 294920 | tf_op jit(solution)/shard_map/ppermute | solution.py:21
Sparse Core Ops, SparseCore 0:
  25.8 43.2 all-gather.5
  70.8 85.7 all-gather.3
where the time goes:
time: 272 us; the launch traced here: 270 us
  waiting for transfers between devices  115 us (42%)
  local copies, waits for them, and re-layouts  35.4 us (13%)
  matrix products  34.9 us (13%)
  blocking collectives  30.8 us (11%)
  starting transfers between devices  27.2 us (10%)
  between operations  13.8 us (5%)
  other arithmetic  13.6 us (5%)
    all_to_all x1, waiting for transfers between devices, shards(): lax.all_to_all(outgoing, 'trk', split_axis=0, concat_axis=0, tiled=True)  58.3 us
    all_to_all x1, waiting for transfers between devices, shards(): lax.all_to_all(stored_tiles, 'seq', split_axis=1, concat_axis=0, tiled=True)  52.4 us
    all_to_all x1, blocking collectives, shards(): lax.all_to_all(d_logits.reshape(n_trk, bins, own_tracks), 'trk', split_ax...  30.8 us
    unnamed x18, local copies, waits for them, and re-layouts  11.1 us
    dot_general x1, matrix products, shards(): jnp.dot(rows.reshape(n_trk * bins, width), head_weight, preferred_element...  11 us
    ppermute x2, starting transfers between devices, with_halo(): before = lax.ppermute(last, axis, up)  8.96 us
    dot_general x1, matrix products, shards(): jnp.einsum('qnp,enp->nqe', local_grads.reshape(bins, n_trk, own_tracks),...  8.76 us
    all_to_all x1, starting transfers between devices, shards(): lax.all_to_all(stored_tiles, 'seq', split_axis=1, concat_axis=0, tiled=True)  8.59 us
  transfers between devices with their start and end apart: 8, of which 4 were waited for; matrix products, arithmetic and copies ran while one was open for 23% of the time, Pallas kernels for 0%

commit v1 on v0

v1 whole, which is shorter than its diff:
```python
import jax
import jax.numpy as jnp
import numpy as np
from jax import lax
from jax.sharding import PartitionSpec as P

DILATION_STEP = 64
ROOM = 24

SQRT_HALF = 0.7071067811865476
INV_SQRT_TAU = 0.3989422804014327

SEQ = ("z", "y")
TRK = ("x", "core")


def halo(value, width):
    size = lax.axis_size(SEQ)
    up = [(i, i + 1) for i in range(size - 1)]
    down = [(j, i) for i, j in up]
    before = lax.ppermute(value[value.shape[0] - width :], SEQ, up)
    after = lax.ppermute(value[:width], SEQ, down)
    return before, after


def gelu_exact(v):
    return 0.5 * v * (1.0 + lax.erf(v * SQRT_HALF))


def gelu_slope(v):
    return 0.5 * (1.0 + lax.erf(v * SQRT_HALF)) + v * jnp.exp(-0.5 * v * v) * INV_SQRT_TAU


def core_swap(value):
    return lax.ppermute(value, "core", [(0, 1), (1, 0)])


def shards(
    inputs,
    layernorm_gain,
    dilated_weight,
    mix_weight,
    head_weight,
    head_bias,
    stored_tiles,
    slot_tiles,
):
    n_q = lax.axis_size(SEQ)
    n_x = lax.axis_size("x")
    n_c = lax.axis_size("core")
    x_index = lax.axis_index("x")
    core = lax.axis_index("core")
    bins, width = inputs.shape[1:]
    half = bins // n_c
    tracks = head_weight.shape[1] * n_x * n_c
    slots, _, tile = stored_tiles.shape
    spans = tracks // tile
    depth = n_q * n_c * slots
    want = n_c * spans

    full_head = lax.all_gather(head_weight, TRK, axis=1, tiled=True)
    full_bias = lax.all_gather(head_bias, TRK, axis=0, tiled=True)

    outbound = (
        stored_tiles.reshape(slots, n_q, n_c, half, tile)
        .transpose(1, 2, 0, 3, 4)
        .reshape(depth, half, tile)
    )
    pieces = lax.all_to_all(outbound, ("z", "y", "core"), 0, 0, tiled=True)

    table = slot_tiles.reshape(n_q, n_x, n_c * slots).transpose(1, 0, 2).reshape(n_x, depth)
    dest = jnp.where(table >= 0, table // want, n_x)
    chips = jnp.arange(n_x, dtype=jnp.int32)
    marks = dest[:, :, None] == chips[None, None, :]
    place = jnp.arange(depth, dtype=jnp.int32)
    same = dest[:, :, None] == dest[:, None, :]
    rank = jnp.sum(same & (place[None, None, :] < place[None, :, None]), axis=2, dtype=jnp.int32)
    fullest = jnp.max(jnp.sum(marks, axis=1, dtype=jnp.int32))
    my_dest = lax.dynamic_index_in_dim(dest, x_index, 0, keepdims=False)
    my_rank = lax.dynamic_index_in_dim(rank, x_index, 0, keepdims=False)

    def source(first, count):
        order = first + jnp.arange(count, dtype=jnp.int32)
        hit = (my_dest[None, None, :] == chips[:, None, None]) & (
            my_rank[None, None, :] == order[None, :, None]
        )
        return jnp.sum(hit * place, axis=2, dtype=jnp.int32).reshape(-1)

    sent = jnp.take(pieces, source(0, ROOM), axis=0, mode="clip")
    arrived = lax.all_to_all(sent, "x", 0, 0, tiled=True)

    tiles_wanted = (
        (x_index * n_c + jnp.stack([core, 1 - core]))[:, None] * spans
        + jnp.arange(spans, dtype=jnp.int32)[None, :]
    ).reshape(-1)
    found = tiles_wanted[:, None, None] == table[None]
    came = jnp.where(
        rank < ROOM,
        chips[:, None] * ROOM + rank,
        n_x * ROOM + chips[:, None] * (want - ROOM) + rank - ROOM,
    )
    where = jnp.sum(found * came[None], axis=(1, 2), dtype=jnp.int32)

    def roomy(arrived, pieces, where):
        return jnp.take(arrived, where, axis=0, mode="clip")

    def crowded(arrived, pieces, where):
        more = jnp.take(pieces, source(ROOM, want - ROOM), axis=0, mode="clip")
        rest = lax.all_to_all(more, "x", 0, 0, tiled=True)
        return jnp.take(jnp.concatenate([arrived, rest]), where, axis=0, mode="clip")

    target = lax.cond(fullest > ROOM, crowded, roomy, arrived, pieces, where)
    target = target.reshape(n_c, spans, half, tile).transpose(0, 2, 1, 3).reshape(bins, tracks)

    x_rows = inputs[0].astype(jnp.float32)
    centre_offset = x_rows - jnp.mean(x_rows, axis=1, keepdims=True)
    inverse_deviation = lax.rsqrt(
        jnp.mean(centre_offset * centre_offset, axis=1, keepdims=True) + 1e-05
    )
    centred_normalized = centre_offset * inverse_deviation
    normalized_rows = centred_normalized * layernorm_gain
    activated_rows = gelu_exact(normalized_rows).astype(jnp.bfloat16)
    before, after = halo(activated_rows, DILATION_STEP)
    padded_input = jnp.concatenate([before, activated_rows, after])
    preactivation = jnp.zeros((bins, dilated_weight.shape[2]), jnp.float32)
    for tap in range(3):
        preactivation = preactivation + jnp.dot(
            padded_input[tap * DILATION_STEP : tap * DILATION_STEP + bins],
            dilated_weight[tap],
            preferred_element_type=jnp.float32,
        )
    inner = gelu_exact(preactivation).astype(jnp.bfloat16)
    embed = (x_rows + jnp.dot(inner, mix_weight, preferred_element_type=jnp.float32)).astype(
        jnp.bfloat16
    )
    halves = embed.reshape(n_c, half, width)
    mine = lax.dynamic_index_in_dim(halves, core, 0, keepdims=False)
    theirs = lax.dynamic_index_in_dim(halves, 1 - core, 0, keepdims=False)
    rows = jnp.concatenate([mine, core_swap(theirs)])

    logits = jnp.dot(rows, full_head, preferred_element_type=jnp.float32) + full_bias
    pred = jax.nn.softplus(logits)
    d_logits = ((1.0 - target.astype(jnp.float32) / pred) * jax.nn.sigmoid(logits)).astype(
        jnp.bfloat16
    )
    d_rows = lax.dot_general(
        d_logits, full_head, (((1,), (1,)), ((), ())), preferred_element_type=jnp.float32
    )
    kept = d_rows[:half]
    back = core_swap(d_rows[half:])
    d_embed = jnp.where(
        core == 0, jnp.concatenate([kept, back]), jnp.concatenate([back, kept])
    )
    d_half = d_embed.astype(jnp.bfloat16)
    d_inner = lax.dot_general(
        d_half, mix_weight, (((1,), (1,)), ((), ())), preferred_element_type=jnp.float32
    )
    preact_gradient = (d_inner * gelu_slope(preactivation)).astype(jnp.bfloat16)
    before, after = halo(preact_gradient, DILATION_STEP)
    padded_gradient = jnp.concatenate([before, preact_gradient, after])
    d_act = jnp.zeros((bins, width), jnp.float32)
    for tap in range(3):
        start = (2 - tap) * DILATION_STEP
        d_act = d_act + lax.dot_general(
            padded_gradient[start : start + bins],
            dilated_weight[tap],
            (((1,), (1,)), ((), ())),
            preferred_element_type=jnp.float32,
        )
    scaled_rows = d_act * gelu_slope(normalized_rows) * layernorm_gain
    backward_fn = (
        scaled_rows
        - jnp.mean(scaled_rows, axis=1, keepdims=True)
        - centred_normalized * jnp.mean(scaled_rows * centred_normalized, axis=1, keepdims=True)
    )
    return (d_embed + inverse_deviation * backward_fn)[None]


def solution(mesh):
    chips = jax.sharding.Mesh(
        np.asarray(mesh.devices).reshape(4, 4, 4, 2), ("z", "y", "x", "core")
    )
    in_specs = (
        P(TRK, SEQ, None),
        P(),
        P(),
        P(),
        P(None, TRK),
        P(TRK),
        P(SEQ + TRK, None, None),
        P(),
    )
    out_specs = P(TRK, SEQ, None)
    return jax.shard_map(
        shards, mesh=chips, in_specs=in_specs, out_specs=out_specs, check_vma=False
    )
```

time: 272 us -> 189 us (0.69)
  waiting for transfers between devices: 115 us -> 37.1 us
  local copies, waits for them, and re-layouts: 35.4 us -> 30.8 us
  blocking collectives: 30.8 us -> 26.7 us
    all_to_all x2, waiting for transfers between devices: 111 us -> 29.7 us  [the longest x1 29.7 us: shards(): pieces = lax.all_to_all(outbound, ('z', 'y', 'core'), 0, 0, tiled=True)]
    all_to_all x1 -> x0, blocking collectives: 30.8 us -> none  [shards(): lax.all_to_all(d_logits.reshape(n_trk, bins, own_tracks), 'trk', split_ax...]
    all_gather x0 -> x1, blocking collectives: none -> 26.7 us  [shards(): full_bias = lax.all_gather(head_bias, TRK, axis=0, tiled=True)]
    unnamed x18 -> x28, local copies, waits for them, and re-layouts: 11.1 us -> 2.07 us
    reshape x1 -> x3, local copies, waits for them, and re-layouts: 0.1 us -> 6.25 us  [the longest x1 4.7 us: shards(): stored_tiles.reshape(slots, n_q, n_c, half, tile).transpose(1, 2, 0, 3, 4)]
    all_to_all x2 -> x0, local copies, waits for them, and re-layouts: 5.12 us -> none  [shards(): lax.all_to_all(stored_tiles, 'seq', split_axis=1, concat_axis=0, tiled=True)]
    select_n x7 -> x2, other arithmetic: 4.64 us -> 0.71 us  [the longest x1 0.7 us: shards(): jnp.where(rank < ROOM, chips[:, None] * ROOM + rank, n_x * ROOM + chips[:...]
    scatter x2 -> x0, local copies, waits for them, and re-layouts: 3.4 us -> none  [the longest x1 2.63 us: shards(): lookup = jnp.zeros((n_tiles,), jnp.int32).at[safe].set(arrival, mode='drop')]
  transfers between devices with their start and end apart: 8 -> 9, of which waited for: 4 -> 3; matrix products, arithmetic and copies ran while one was open for 23% -> 26% of each run, Pallas kernels for 0% -> 0%
where the time goes in v1:
time: 189 us; the launch traced here: 187 us
  waiting for transfers between devices  37.1 us (20%)
  matrix products  35.8 us (19%)
  local copies, waits for them, and re-layouts  30.8 us (16%)
  starting transfers between devices  29.8 us (16%)
  blocking collectives  26.7 us (14%)
  between operations  14.4 us (8%)
  other arithmetic  12 us (6%)
    all_to_all x1, waiting for transfers between devices, shards(): pieces = lax.all_to_all(outbound, ('z', 'y', 'core'), 0, 0, tiled=True)  29.7 us
    all_gather x1, blocking collectives, shards(): full_bias = lax.all_gather(head_bias, TRK, axis=0, tiled=True)  26.7 us
    dot_general x1, matrix products, shards(): lax.dot_general(d_logits, full_head, (((1,), (1,)), ((), ())), preferred_...  15.8 us
    ppermute x2, starting transfers between devices, halo(): before = lax.ppermute(value[value.shape[0] - width:], SEQ, up)  9.85 us
    dot_general x3, matrix products, shards(): lax.dot_general(padded_gradient[start:start + bins], dilated_weight[tap],...  8.24 us
    all_to_all x1, starting transfers between devices, shards(): pieces = lax.all_to_all(outbound, ('z', 'y', 'core'), 0, 0, tiled=True)  8.06 us
    dot_general x3, matrix products, shards(): jnp.dot(padded_input[tap * DILATION_STEP:tap * DILATION_STEP + bins], dil...  7.98 us
    gather x1, local copies, waits for them, and re-layouts, shards(): sent = jnp.take(pieces, source(0, ROOM), axis=0, mode='clip')  5.12 us
  transfers between devices with their start and end apart: 9, of which 3 were waited for; matrix products, arithmetic and copies ran while one was open for 26% of the time, Pallas kernels for 0%

profile of v1, /device:TPU:56, one launch (start us, length us, event | category | flops | bytes accessed | tf_op | source)
XLA Modules:
  0.0 186.6 jit_solution(11957815026773629478)
XLA Ops:
  7.3 4.7 %copy.18 = bf16[4,16,2,128,128]{4,3,0,2,1:T(8,128)(2,1)} copy(bf16[4,16,2,128,128]{4,3,2,1,0:T(8,128)(2,1)} %bitcast.121) | data formatting | bytes 8388608 | tf_op jit(solution)/shard_map/reshape | solution.py:65
  12.0 8.1 %all-to-all-start.1 = ((bf16[128,128,128]{2,1,0:T(8,128)(2,1)}), bf16[128,128,128]{2,1,0:T(8,128)(2,1)}, u32[]{:S(2)}, u32[]{:S(2)}) async-start(bf16[128,128,128]{2,1,0:T(8,128)(2,1)} %bitcast.118), calls=%async_computation.1 | async-start | bytes 8388608 | tf_op jit(solution)/shard_map/all_to_all | solution.py:69
  22.7 2.8 %collective-permute-start.1 = (bf16[64,1536]{1,0:T(8,128)(2,1)S(1)}, bf16[64,1536]{1,0:T(8,128)(2,1)}, u32[]{:S(2)}, u32[]{:S(2)}) collective-permute-start(bf16[64,1536]{1,0:T(8,128)(2,1)S(1)} %get-tuple-element.42), channel_id=1, source_target_pairs={{8,0},{16,8},{24,16},{32,24},{40,32},{48,40},{56,48},{64,56},{72,6... | collective-permute-start | bytes 589832 | tf_op jit(solution)/shard_map/ppermute | solution.py:22
  25.5 5.2 %collective-permute-start = (bf16[64,1536]{1,0:T(8,128)(2,1)S(1)}, bf16[64,1536]{1,0:T(8,128)(2,1)}, u32[]{:S(2)}, u32[]{:S(2)}) collective-permute-start(bf16[64,1536]{1,0:T(8,128)(2,1)S(1)} %get-tuple-element.41), channel_id=1, source_target_pairs={{0,8},{8,16},{16,24},{24,32},{32,40},{40,48},{48,56},{56,64},{64,7... | collective-permute-start | bytes 589832 | tf_op jit(solution)/shard_map/ppermute | solution.py:21
  38.5 29.7 %all-to-all-done.1 = bf16[128,128,128]{2,1,0:T(8,128)(2,1)} async-done(((bf16[128,128,128]{2,1,0:T(8,128)(2,1)}), bf16[128,128,128]{2,1,0:T(8,128)(2,1)}, u32[]{:S(2)}, u32[]{:S(2)}) %all-to-all-start.1) | async-done | bytes 4194336 | tf_op jit(solution)/shard_map/all_to_all | solution.py:69
  68.2 5.1 %gather_fusion.3 = bf16[96,128,128]{2,1,0:T(8,128)(2,1)} fusion(bf16[128,128,128]{2,1,0:T(8,128)(2,1)} %all-to-all-done.1, s32[1024]{0:T(1024)} %pad_clamp_fusion.3), kind=kCustom, calls=%fused_computation.3 | custom fusion | bytes 6291840 | tf_op jit(solution)/shard_map/jit(_take)/gather | solution.py:89
  73.4 4.8 %all-to-all-start.2 = ((bf16[96,128,128]{2,1,0:T(8,128)(2,1)}), bf16[96,128,128]{2,1,0:T(8,128)(2,1)}, u32[]{:S(2)}, u32[]{:S(2)}) async-start(bf16[96,128,128]{2,1,0:T(8,128)(2,1)} %gather_fusion.3), calls=%async_computation.2 | async-start | bytes 6291456 | tf_op jit(solution)/shard_map/all_to_all | solution.py:90
  78.8 2.8 %fusion.14 = f32[256,768]{1,0:T(8,128)S(1)} fusion(bf16[3,1536,768]{2,1,0:T(8,128)(2,1)} %param.12, bf16[1,256,1536]{2,1,0:T(8,128)(2,1)S(1)} %copy-done.1, f32[1536]{0:T(1024)} %param.11, f32[256]{0:T(256)S(1)} %copy-done.6, f32[256]{0:T(256)S(1)} %broadcast_multiply_fusion.2), kind=kOutput, calls=%fused_computation.34 | convolution fusion | flops 607518720 | bytes 3942400 | tf_op jit(solution)/shard_map/dot_general | solution.py:127
  82.4 2.6 %fusion.10 = f32[256,768]{1,0:T(8,128)S(1)} fusion(bf16[3,1536,768]{2,1,0:T(8,128)(2,1)} %param.12, bf16[64,1536]{1,0:T(8,128)(2,1)} %collective-permute-done.1, bf16[256,1536]{1,0:T(8,128)(2,1)S(1)} %copy-done.4), kind=kOutput, calls=%fused_computation.30 | convolution fusion | flops 605552640 | bytes 4128768 | tf_op jit(solution)/shard_map/dot_general | solution.py:127
  85.0 2.6 %fusion.62 = f32[256,768]{1,0:T(8,128)S(1)} fusion(f32[256,768]{1,0:T(8,128)S(1)} %fusion.10, f32[256,768]{1,0:T(8,128)S(1)} %fusion.14, bf16[3,1536,768]{2,1,0:T(8,128)(2,1)} %param.12, bf16[256,1536]{1,0:T(8,128)(2,1)S(1)} %copy-done.4, bf16[64,1536]{1,0:T(8,128)(2,1)} %collective-permute-done), kind=kOutput, calls=%fused_computation.81 | convolution fusion | flops 605945856 | bytes 5701632 | tf_op jit(solution)/shard_map/dot_general | solution.py:127
  95.3 26.7 %all-gather = f32[8,1,512]{2,1,0:T(1,128)} all-gather(f32[1,1,512]{2,1,0:T(1,128)} %bitcast.125), channel_id=1, replica_groups=mesh['z'=4,'y'=4,'x'=4,'core'=2] {'x','core'}, dimensions={0}, use_global_device_ids=true | all-gather | bytes 18432 | tf_op jit(solution)/shard_map/all_gather | solution.py:62
  124.7 4.0 %conditional.1 = (bf16[64,128,128]{2,1,0:T(8,128)(2,1)}) conditional(s32[]{:T(128)} %convert_element_type.55, (s32[64]{0:T(128)S(1)}, bf16[96,128,128]{2,1,0:T(8,128)(2,1)}) %tuple.11, (s32[128]{0:T(128)}, s32[4]{0:T(128)}, s32[128]{0:T(128)}, s32[128]{0:T(128)}, bf16[128,128,128]{2,1,0:T(8,128)(2,1)}, /*index=5*/bf16[96,128,128]{2,1,0:T(8,128)(2,1)}, ...), branch_computations={%region_5.6_spmd, %region_6.8_spmd} | conditional | flops 4263304 | bytes 47211000 | solution.py:112
  124.7 4.0 %gather_fusion = bf16[64,128,128]{2,1,0:T(8,128)(2,1)} fusion(bf16[96,128,128]{2,1,0:T(8,128)(2,1)} %get-tuple-element.26, s32[1024]{0:T(1024)S(1)} %pad_clamp_fusion), kind=kCustom, calls=%fused_computation | custom fusion | bytes 4194560 | tf_op jit(solution)/shard_map/cond/branch_0_fun/jit(_take)/gather | solution.py:105
  128.7 4.7 %copy.19 = f32[2,32,128,128]{3,1,2,0:T(8,128)} copy(bf16[2,32,128,128]{3,2,1,0:T(8,128)(2,1)} %bitcast.119) | data formatting | bytes 6291456 | tf_op jit(solution)/shard_map/convert_element_type | solution.py:143
  133.5 15.8 %fusion.19 = f32[256,1536]{1,0:T(8,128)} fusion(bf16[1536,4096]{1,0:T(8,128)(2,1)} %all-gather.3.cloned.1.call-done, f32[32,8,32,128]{3,2,1,0:T(8,128)} %bitcast.120, f32[4096]{0:T(1024)} %bitcast.124, bf16[128,1536]{1,0:T(8,128)(2,1)} %collective-permute-done.2, bf16[128,1536]{1,0:T(8,128)(2,1)S(1)} %get-tuple-element.39), kind=kOutput, calls=%fused_computation.39 | convolution fusion | flops 6458703872 | bytes 19152896 | tf_op jit(solution)/shard_map/dot_general | solution.py:146
  149.2 2.6 %fusion.112 = (f32[128,1536]{1,0:T(8,128)}, f32[128,1536]{1,0:T(8,128)}) fusion(f32[256,1536]{1,0:T(8,128)} %fusion.19), kind=kLoop, calls=%fused_computation.158 | loop fusion | bytes 3145728 | tf_op jit(solution)/shard_map/slice | solution.py:150
  152.1 2.3 %collective-permute-done.3 = f32[128,1536]{1,0:T(8,128)} collective-permute-done((f32[128,1536]{1,0:T(8,128)}, f32[128,1536]{1,0:T(8,128)}, u32[]{:S(2)}, u32[]{:S(2)}) %collective-permute-start.3) | collective-permute-done | bytes 786464 | tf_op jit(solution)/shard_map/ppermute | solution.py:35
  154.5 3.0 %fusion.65 = bf16[256,768]{1,0:T(8,128)(2,1)S(1)} fusion(bf16[768,1536]{1,0:T(8,128)(2,1)S(1)} %copy-done, f32[128,1536]{1,0:T(8,128)} %get-tuple-element.38, f32[128,1536]{1,0:T(8,128)} %collective-permute-done.3, f32[256,768]{1,0:T(8,128)} %copy-done.13, pred[]{:T(512)S(6)} %eq.116), kind=kOutput, calls=%fused_computation.83 | convolution fusion | flops 609484800 | bytes 5111809 | tf_op jit(solution)/shard_map/dot_general | solution.py:155
  157.5 4.7 %collective-permute-start.5 = (bf16[64,768]{1,0:T(8,128)(2,1)S(1)}, bf16[64,768]{1,0:T(8,128)(2,1)S(1)}, u32[]{:S(2)}, u32[]{:S(2)}) collective-permute-start(bf16[64,768]{1,0:T(8,128)(2,1)S(1)} %get-tuple-element.44), channel_id=1, source_target_pairs={{0,8},{8,16},{16,24},{24,32},{32,40},{40,48},{48,56},{56,64},{64,7... | collective-permute-start | bytes 294920 | tf_op jit(solution)/shard_map/ppermute | solution.py:21
  162.2 2.5 %fusion.12 = f32[256,1536]{1,0:T(8,128)S(1)} fusion(bf16[256,768]{1,0:T(8,128)(2,1)S(1)} %fusion.65, bf16[3,1536,768]{2,1,0:T(8,128)(2,1)} %param.12), kind=kOutput, calls=%fused_computation.32 | convolution fusion | flops 603979776 | bytes 4325376 | tf_op jit(solution)/shard_map/dot_general | solution.py:164
  166.6 2.5 %fusion.8 = f32[256,1536]{1,0:T(8,128)S(1)} fusion(bf16[3,1536,768]{2,1,0:T(8,128)(2,1)} %param.12, bf16[256,768]{1,0:T(8,128)(2,1)S(1)} %fusion.65, bf16[64,768]{1,0:T(8,128)(2,1)S(1)} %collective-permute-done.5), kind=kOutput, calls=%fused_computation.28 | convolution fusion | flops 604766208 | bytes 4423680 | tf_op jit(solution)/shard_map/dot_general | solution.py:164
  169.1 4.3 %collective-permute-done.4 = bf16[64,768]{1,0:T(8,128)(2,1)S(1)} collective-permute-done((bf16[64,768]{1,0:T(8,128)(2,1)S(1)}, bf16[64,768]{1,0:T(8,128)(2,1)S(1)}, u32[]{:S(2)}, u32[]{:S(2)}) %collective-permute-start.4) | collective-permute-done | bytes 98336 | tf_op jit(solution)/shard_map/ppermute | solution.py:22
  173.4 3.3 %fusion.111 = (f32[256]{0:T(256)S(1)}, f32[256]{0:T(256)S(1)}, f32[256,1536]{1,0:T(8,128)S(1)}) fusion(f32[256]{0:T(256)S(1)} %copy-done.6, f32[256]{0:T(256)S(1)} %broadcast_multiply_fusion.2, bf16[1,256,1536]{2,1,0:T(8,128)(2,1)S(1)} %copy-done.1, f32[1536]{0:T(1024)S(1)} %copy-done.8, f32[256,1536]{1,0:T(8,128)S(1)} %fusion.8, ...), kind=kOutput, calls=%fused_computation.157 | convolution fusion | flops 612236800 | bytes 8366080 | tf_op jit(solution)/shard_map/dot_general | solution.py:164
  176.7 3.1 %fusion.48 = f32[1,256,1536]{2,1,0:T(8,128)} fusion(bf16[1,256,1536]{2,1,0:T(8,128)(2,1)S(1)} %copy-done.1, f32[256,1536]{1,0:T(8,128)S(1)} %get-tuple-element.45, f32[128,1536]{1,0:T(8,128)S(1)} %copy-done.2, f32[128,1536]{1,0:T(8,128)} %collective-permute-done.3, f32[256]{0:T(256)S(1)} %broadcast_multiply_fusion, f32[256]{0:T(256)S(1)} %broadcast_multiply_fusion.1, ...), kind=kLoop, calls=%fused_computation.68 | loop fusion | flops 4325376 | bytes 5509121 | tf_op jit(solution)/shard_map/broadcast_in_dim | solution.py:176
  (73 shorter events, 24.4 us)
Async XLA Ops:
  6.5 81.0 %copy-start = (bf16[768,1536]{1,0:T(8,128)(2,1)S(1)}, bf16[768,1536]{1,0:T(8,128)(2,1)}, u32[]{:S(2)}) copy-start(bf16[768,1536]{1,0:T(8,128)(2,1)} %param.13) | copy-start | bytes 7077892
  6.5 126.9 %all-gather.3.cloned.1.call-start = ((), (), s32[]{:S(2)}) async-start(), calls=%async_computation.3 | async-start | bytes 14155776 | tf_op jit(solution)/shard_map/all_gather | solution.py:61
  12.0 8.1 %copy-start.1 = (bf16[1,256,1536]{2,1,0:T(8,128)(2,1)S(1)}, bf16[1,256,1536]{2,1,0:T(8,128)(2,1)}, u32[]{:S(2)}) copy-start(bf16[1,256,1536]{2,1,0:T(8,128)(2,1)} %param.10) | copy-start | bytes 2359300
  12.0 56.3 %all-to-all-start.1 = ((bf16[128,128,128]{2,1,0:T(8,128)(2,1)}), bf16[128,128,128]{2,1,0:T(8,128)(2,1)}, u32[]{:S(2)}, u32[]{:S(2)}) async-start(bf16[128,128,128]{2,1,0:T(8,128)(2,1)} %bitcast.118), calls=%async_computation.1 | async-start | bytes 8388608 | tf_op jit(solution)/shard_map/all_to_all | solution.py:69
  20.0 1.2 copy-start.7
  20.2 10.5 %copy-start.10 = (s32[512]{0:T(512)S(1)}, s32[512]{0:T(512)}, u32[]{:S(2)}) copy-start(s32[512]{0:T(512)} %param.17) | copy-start | bytes 6148
  20.6 0.6 copy-start.5
  21.8 0.9 copy-start.3
  22.7 59.7 %collective-permute-start.1 = (bf16[64,1536]{1,0:T(8,128)(2,1)S(1)}, bf16[64,1536]{1,0:T(8,128)(2,1)}, u32[]{:S(2)}, u32[]{:S(2)}) collective-permute-start(bf16[64,1536]{1,0:T(8,128)(2,1)S(1)} %get-tuple-element.42), channel_id=1, source_target_pairs={{8,0},{16,8},{24,16},{32,24},{40,32},{48,40},{56,48},{64,56},{72,6... | collective-permute-start | bytes 589832 | tf_op jit(solution)/shard_map/ppermute | solution.py:22
  25.5 59.5 %collective-permute-start = (bf16[64,1536]{1,0:T(8,128)(2,1)S(1)}, bf16[64,1536]{1,0:T(8,128)(2,1)}, u32[]{:S(2)}, u32[]{:S(2)}) collective-permute-start(bf16[64,1536]{1,0:T(8,128)(2,1)S(1)} %get-tuple-element.41), channel_id=1, source_target_pairs={{0,8},{8,16},{16,24},{24,32},{32,40},{40,48},{48,56},{56,64},{64,7... | collective-permute-start | bytes 589832 | tf_op jit(solution)/shard_map/ppermute | solution.py:21
  33.9 0.5 copy-start.11
  33.9 0.5 copy-start.9
  73.4 5.5 %copy-start.6 = (f32[256]{0:T(256)S(1)}, f32[256]{0:T(256)}, u32[]{:S(2)}) copy-start(f32[256]{0:T(256)} %copy-done.5) | copy-start | bytes 3076
  73.4 50.1 %all-to-all-start.2 = ((bf16[96,128,128]{2,1,0:T(8,128)(2,1)}), bf16[96,128,128]{2,1,0:T(8,128)(2,1)}, u32[]{:S(2)}, u32[]{:S(2)}) async-start(bf16[96,128,128]{2,1,0:T(8,128)(2,1)} %gather_fusion.3), calls=%async_computation.2 | async-start | bytes 6291456 | tf_op jit(solution)/shard_map/all_to_all | solution.py:90
  78.8 2.9 %copy-start.12 = (s32[2]{0:T(128)S(1)}, s32[2]{0:T(128)}, u32[]{:S(2)}) copy-start(s32[2]{0:T(128)} %fusion.97) | copy-start | bytes 28
  78.8 3.5 %copy-start.4 = (bf16[256,1536]{1,0:T(8,128)(2,1)S(1)}, bf16[256,1536]{1,0:T(8,128)(2,1)}, u32[]{:S(2)}) copy-start(bf16[256,1536]{1,0:T(8,128)(2,1)} %copy-done.3) | copy-start | bytes 2359300
  87.5 0.9 copy-start.13
  89.2 44.3 %collective-permute-start.2 = (bf16[128,1536]{1,0:T(8,128)(2,1)}, bf16[128,1536]{1,0:T(8,128)(2,1)}, u32[]{:S(2)}, u32[]{:S(2)}) collective-permute-start(bf16[128,1536]{1,0:T(8,128)(2,1)} %get-tuple-element.40), channel_id=1, source_target_pairs={{0,1},{1,0},{2,3},{3,2},{4,5},{5,4},{6,7},{7,6},{8,9},{9,8},{10,11... | collective-permute-start | bytes 1179656 | tf_op jit(solution)/shard_map/ppermute | solution.py:35
  151.8 2.6 %collective-permute-start.3 = (f32[128,1536]{1,0:T(8,128)}, f32[128,1536]{1,0:T(8,128)}, u32[]{:S(2)}, u32[]{:S(2)}) collective-permute-start(f32[128,1536]{1,0:T(8,128)} %get-tuple-element.37), channel_id=1, source_target_pairs={{0,1},{1,0},{2,3},{3,2},{4,5},{5,4},{6,7},{7,6},{8,9},{9,8},{10,11... | collective-permute-start | bytes 2359304 | tf_op jit(solution)/shard_map/ppermute | solution.py:35
  157.5 9.1 %collective-permute-start.5 = (bf16[64,768]{1,0:T(8,128)(2,1)S(1)}, bf16[64,768]{1,0:T(8,128)(2,1)S(1)}, u32[]{:S(2)}, u32[]{:S(2)}) collective-permute-start(bf16[64,768]{1,0:T(8,128)(2,1)S(1)} %get-tuple-element.44), channel_id=1, source_target_pairs={{0,8},{8,16},{16,24},{24,32},{32,40},{40,48},{48,56},{56,64},{64,7... | collective-permute-start | bytes 294920 | tf_op jit(solution)/shard_map/ppermute | solution.py:21
  164.6 8.7 %copy-start.8 = (f32[1536]{0:T(1024)S(1)}, f32[1536]{0:T(1024)}, u32[]{:S(2)}) copy-start(f32[1536]{0:T(1024)} %param.11) | copy-start | bytes 18436
  164.7 8.7 %collective-permute-start.4 = (bf16[64,768]{1,0:T(8,128)(2,1)S(1)}, bf16[64,768]{1,0:T(8,128)(2,1)S(1)}, u32[]{:S(2)}, u32[]{:S(2)}) collective-permute-start(bf16[64,768]{1,0:T(8,128)(2,1)S(1)} %get-tuple-element.43), channel_id=1, source_target_pairs={{8,0},{16,8},{24,16},{32,24},{40,32},{48,40},{56,48},{64,56},{72,6... | collective-permute-start | bytes 294920 | tf_op jit(solution)/shard_map/ppermute | solution.py:22
  169.1 7.6 %copy-start.2 = (f32[128,1536]{1,0:T(8,128)S(1)}, f32[128,1536]{1,0:T(8,128)}, u32[]{:S(2)}) copy-start(f32[128,1536]{1,0:T(8,128)} %get-tuple-element.38) | copy-start | bytes 2359300
Sparse Core Ops, SparseCore 0:
  9.1 68.9 all-gather.2

commit v2 on v1

v2 whole, which is shorter than its diff:
```python
import jax
import jax.numpy as jnp
import numpy as np
from jax import lax
from jax.experimental import pallas as pl
from jax.experimental.pallas import tpu as pltpu
from jax.sharding import PartitionSpec as P

DILATION_STEP = 64
ROOM = 24
SPARE = 8
LEAD = 12

SQRT_HALF = 0.7071067811865476
INV_SQRT_TAU = 0.3989422804014327

SEQ = ("z", "y")
TRK = ("x", "core")


def halo(last, first):
    size = lax.axis_size(SEQ)
    up = [(i, i + 1) for i in range(size - 1)]
    down = [(j, i) for i, j in up]
    return lax.ppermute(last, SEQ, up), lax.ppermute(first, SEQ, down)


def core_swap(value):
    return lax.ppermute(value, "core", [(0, 1), (1, 0)])


ANY = pl.BlockSpec(memory_space=pl.ANY)
FREE = pl.CostEstimate(flops=0, bytes_accessed=0, transcendentals=0)


def room(mib):
    return pltpu.CompilerParams(vmem_limit_bytes=mib * 1024 * 1024)


def nt_dot(a, b):
    return lax.dot_general(a, b, (((1,), (1,)), ((), ())), preferred_element_type=jnp.float32)


def arrange(stored, parts, after):
    slots, bins, tile = stored.shape
    each = bins // parts

    def kernel(in_ref, *rest):
        out_ref, held, into, out = rest[len(after) :]
        reads = [pltpu.make_async_copy(in_ref.at[s], held.at[s], into.at[s]) for s in range(slots)]
        writes = [
            pltpu.make_async_copy(held.at[s], out_ref.at[:, s], out.at[s]) for s in range(slots)
        ]
        for read in reads:
            read.start()
        for read, write in zip(reads, writes):
            read.wait()
            write.start()
        for write in writes:
            write.wait()

    return pl.pallas_call(
        kernel,
        out_shape=jax.ShapeDtypeStruct((parts, slots, each, tile), stored.dtype),
        in_specs=[ANY] * (1 + len(after)),
        out_specs=ANY,
        scratch_shapes=[
            pltpu.VMEM((slots, parts, each, tile), stored.dtype),
            pltpu.SemaphoreType.DMA((slots,)),
            pltpu.SemaphoreType.DMA((slots,)),
        ],
        compiler_params=room(56),
        cost_estimate=FREE,
    )(stored.reshape(slots, parts, each, tile), *after)


def head_block(head, bias, extra):
    width, own = head.shape
    full = pl.BlockSpec(memory_space=pltpu.VMEM)

    def kernel(head_ref, bias_ref, out_ref):
        out_ref[:own] = head_ref[...].T
        out_ref[own:] = jnp.zeros((extra, width), head.dtype)
        left = bias_ref[...]
        for part in range(width // own):
            piece = left.astype(jnp.bfloat16)
            left = left - piece.astype(jnp.float32)
            out_ref[own : own + 1, part * own : (part + 1) * own] = piece

    return pl.pallas_call(
        kernel,
        out_shape=jax.ShapeDtypeStruct((own + extra, width), head.dtype),
        in_specs=[full, full],
        out_specs=full,
        compiler_params=room(16),
        cost_estimate=FREE,
    )(head, bias[None])


def norm_pass(before, x, after, gain):
    bins, width = x.shape
    step = before.shape[0]
    full = pl.BlockSpec(memory_space=pltpu.VMEM)

    def kernel(before_ref, x_ref, after_ref, gain_ref, out_ref, xhat_ref, factor_ref, scale_ref):
        chunks = [(before_ref, 0)] + [(x_ref, i) for i in range(0, bins, step)] + [(after_ref, 0)]
        for i, (ref, top) in enumerate(chunks):
            rows = ref[pl.ds(top, step)].astype(jnp.float32)
            offset = rows - jnp.mean(rows, axis=1, keepdims=True)
            scale = lax.rsqrt(jnp.mean(offset * offset, axis=1, keepdims=True) + 1e-05)
            xhat = offset * scale
            v = xhat * gain_ref[...]
            phi = 0.5 * (1.0 + lax.erf(v * SQRT_HALF))
            out_ref[pl.ds(i * step, step)] = (v * phi).astype(jnp.bfloat16)
            if ref is x_ref:
                at = pl.ds(top, step)
                slope = phi + v * jnp.exp(-0.5 * v * v) * INV_SQRT_TAU
                xhat_ref[at] = xhat
                factor_ref[at] = slope * gain_ref[...]
                scale_ref[at] = scale

    wide = jax.ShapeDtypeStruct((bins, width), jnp.float32)
    return pl.pallas_call(
        kernel,
        out_shape=(
            jax.ShapeDtypeStruct((bins + 2 * step, width), jnp.bfloat16),
            wide,
            wide,
            jax.ShapeDtypeStruct((bins, 1), jnp.float32),
        ),
        in_specs=[full] * 4,
        out_specs=(full,) * 4,
        compiler_params=room(12),
        cost_estimate=FREE,
    )(before, x, after, gain[None])


def blank(shape, dtype):
    return pl.pallas_call(
        lambda out_ref: None,
        out_shape=jax.ShapeDtypeStruct(shape, dtype),
        out_specs=ANY,
        cost_estimate=FREE,
    )()


def pick_kernel(count, index_ref, pieces_ref, out_ref, mark_ref, sem):
    def start(i, carry):
        pltpu.make_async_copy(pieces_ref.at[index_ref[i]], out_ref.at[i], sem).start()
        return carry

    lax.fori_loop(0, count, start, 0, unroll=8)
    mark_ref[...] = jnp.zeros_like(mark_ref)
    pltpu.make_async_copy(pieces_ref.at[pl.ds(0, count)], out_ref, sem).wait()


def pick(pieces, index):
    count = index.shape[0]
    block = (count,) + pieces.shape[1:]
    return pl.pallas_call(
        lambda *refs: pick_kernel(count, *refs),
        out_shape=(
            jax.ShapeDtypeStruct(block, pieces.dtype),
            jax.ShapeDtypeStruct((8, 128), jnp.float32),
        ),
        grid_spec=pltpu.PrefetchScalarGridSpec(
            num_scalar_prefetch=1,
            grid=(1,),
            in_specs=[ANY],
            out_specs=(
                pl.BlockSpec(block, lambda i, index: (0, 0, 0)),
                pl.BlockSpec((8, 128), lambda i, index: (0, 0)),
            ),
            scratch_shapes=[pltpu.SemaphoreType.DMA],
        ),
        compiler_params=room(16),
        cost_estimate=FREE,
    )(index, pieces)


def gate(value, *others, lead=0):
    return pl.pallas_call(
        lambda *refs: None,
        out_shape=jax.ShapeDtypeStruct(value.shape, value.dtype),
        in_specs=[ANY] * (1 + len(others)),
        out_specs=ANY,
        input_output_aliases={0: 0},
        cost_estimate=pl.CostEstimate(flops=lead * 10**9, bytes_accessed=0, transcendentals=0),
    )(value, *others)


def fetch(g, blocks, held, sems, go):
    for j, parts in enumerate(blocks):

        @pl.when(g == j)
        def _():
            top = 0
            for part in parts:
                copy = pltpu.make_async_copy(
                    part, held.at[j % 2, pl.ds(top, part.shape[0])], sems.at[j % 2]
                )
                copy.start() if go else copy.wait()
                top += part.shape[0]


def next_block(g, blocks, held, sems):
    @pl.when(g == 0)
    def _():
        fetch(g, blocks, held, sems, True)

    fetch(g, blocks, held, sems, False)
    fetch(g + 1, blocks, held, sems, True)


def nest(flat, counts):
    out = []
    for n in counts:
        out.append(flat[:n])
        flat = flat[n:]
    return out


def forward_kernel(core_ref, act_ref, x_ref, taps_ref, mix_ref, *rest):
    slope_ref, mine_ref, theirs_ref, mark_ref, embed = rest
    mark_ref[...] = jnp.zeros_like(mark_ref)
    bins = x_ref.shape[0]
    step = (act_ref.shape[0] - bins) // 2
    half = mine_ref.shape[0]

    def dot(a, b):
        return jnp.dot(a, b, preferred_element_type=jnp.float32)

    v = dot(act_ref[:bins], taps_ref[0])
    v = v + dot(act_ref[step : step + bins], taps_ref[1])
    v = v + dot(act_ref[2 * step :], taps_ref[2])
    phi = 0.5 * (1.0 + lax.erf(v * SQRT_HALF))
    slope_ref[...] = phi + v * jnp.exp(-0.5 * v * v) * INV_SQRT_TAU
    embed[...] = x_ref[...].astype(jnp.float32) + dot((v * phi).astype(jnp.bfloat16), mix_ref[...])
    at = pl.multiple_of(core_ref[0] * half, half)
    mine_ref[...] = embed[pl.ds(at, half)].astype(jnp.bfloat16)
    theirs_ref[...] = embed[pl.ds(half - at, half)].astype(jnp.bfloat16)


def forward_pass(core, act, x, taps, mix, half):
    bins, width = x.shape
    inner = taps.shape[2]
    out = jax.ShapeDtypeStruct((half, width), jnp.bfloat16)
    full = pl.BlockSpec(memory_space=pltpu.VMEM)
    return pl.pallas_call(
        forward_kernel,
        out_shape=(
            jax.ShapeDtypeStruct((bins, inner), jnp.float32),
            out,
            out,
            jax.ShapeDtypeStruct((8, 128), jnp.float32),
        ),
        in_specs=[pl.BlockSpec(memory_space=pltpu.SMEM)] + [full] * 4,
        out_specs=(full,) * 4,
        scratch_shapes=[pltpu.VMEM((bins, width), jnp.float32)],
        compiler_params=room(18),
        cost_estimate=FREE,
    )(core, act, x, taps, mix)


def head_kernel(counts, own, mine_ref, other_ref, *rest):
    sig_ref, ratio_ref, head_ref, rows, held, sems = rest[-6:]
    g = pl.program_id(0)
    half = mine_ref.shape[0]

    @pl.when(g == 0)
    def _():
        rows[:half] = mine_ref[...]
        rows[half:] = other_ref[...]

    next_block(g, nest(rest[: sum(counts)], counts), held, sems)
    w = held.at[g % 2]
    head_ref[...] = w[:own]
    logits = nt_dot(rows[...], w[:own])
    bias = jnp.sum(w[own:].astype(jnp.float32), axis=0, keepdims=True)
    for part in range(bias.shape[1] // own):
        logits = logits + bias[:, part * own : (part + 1) * own]
    e = jnp.exp(-jnp.abs(logits))
    inverse = 1.0 / (1.0 + e)
    sig = jnp.where(logits >= 0.0, inverse, e * inverse)
    pred = jnp.maximum(logits, 0.0) + jnp.log1p(e)
    sig_ref[...] = sig
    ratio_ref[...] = sig / pred


def head_pass(mine, other, blocks, own, others):
    half, width = mine.shape
    n = 2 * half
    counts = [len(parts) for parts in blocks]
    flat = [part for parts in blocks for part in parts]
    tall = blocks[0][0].shape[0]
    tracks = own * len(blocks)
    out = jax.ShapeDtypeStruct((n, tracks), jnp.float32)
    out_spec = pl.BlockSpec((n, own), lambda g: (0, g))
    row_spec = pl.BlockSpec((half, width), lambda g: (0, 0))
    return pl.pallas_call(
        lambda *refs: head_kernel(counts, own, *refs),
        out_shape=(out, out, jax.ShapeDtypeStruct((tracks, width), mine.dtype)),
        grid=(len(blocks),),
        in_specs=[row_spec, row_spec] + [ANY] * (len(flat) + len(others)),
        out_specs=(out_spec, out_spec, pl.BlockSpec((own, width), lambda g: (g, 0))),
        scratch_shapes=[
            pltpu.VMEM((n, width), jnp.bfloat16),
            pltpu.VMEM((2, tall, width), jnp.bfloat16),
            pltpu.SemaphoreType.DMA((2,)),
        ],
        compiler_params=room(14),
        cost_estimate=FREE,
    )(mine, other, *flat, *others)


def grad_kernel(kinds, own_spans, plan_ref, sig_ref, ratio_ref, *rest):
    sources = rest[:kinds]
    kept_ref, sent_ref, tiles, sems = rest[kinds:]
    half, tile = tiles.shape[1:]
    spans = sig_ref.shape[1] // tile
    per = 2 * own_spans
    usual = kinds // 2 + 1

    def copies(group, go):
        top = sum(source.shape[0] for source in sources[: group[0]])
        for k in group:
            copy = pltpu.make_async_copy(
                sources[k], tiles.at[pl.ds(top, sources[k].shape[0])], sems.at[k]
            )
            copy.start() if go else copy.wait()
            top += sources[k].shape[0]

    copies(range(usual), True)

    @pl.when(plan_ref[2 * spans] > 0)
    def _():
        copies(range(usual, kinds), True)
        copies(range(usual, kinds), False)

    copies(range(usual), False)
    for s, out_ref in enumerate((kept_ref, sent_ref)):
        for k in range(spans):
            cols = pl.ds(k * tile, tile)
            at = (pl.ds(s * half, half), cols)
            spot = plan_ref[k // own_spans * per + s * own_spans + k % own_spans]
            t = tiles[spot].astype(jnp.float32)
            out_ref[:, cols] = (sig_ref[at] - t * ratio_ref[at]).astype(jnp.bfloat16)


def grad_pass(plan, sig, ratio, sources, own_spans):
    n, tracks = sig.shape
    half, tile = sources[0].shape[1:]
    out = jax.ShapeDtypeStruct((half, tracks), jnp.bfloat16)
    full = pl.BlockSpec(memory_space=pltpu.VMEM)
    total = sum(source.shape[0] for source in sources)
    return pl.pallas_call(
        lambda *refs: grad_kernel(len(sources), own_spans, *refs),
        out_shape=(out, out),
        in_specs=[pl.BlockSpec(memory_space=pltpu.SMEM), full, full] + [ANY] * len(sources),
        out_specs=(full, full),
        scratch_shapes=[
            pltpu.VMEM((total, half, tile), jnp.bfloat16),
            pltpu.SemaphoreType.DMA((len(sources),)),
        ],
        compiler_params=room(12),
        cost_estimate=FREE,
    )(plan, sig, ratio, *sources)


def inner_pass(core, kept, back, mix, slope, step):
    half, width = kept.shape
    bins, inner = slope.shape
    full = pl.BlockSpec(memory_space=pltpu.VMEM)

    def kernel(core_ref, kept_ref, back_ref, mix_ref, slope_ref, embed_ref, pre_ref, *ends):
        at = pl.multiple_of(core_ref[0] * half, half)
        embed_ref[pl.ds(at, half)] = kept_ref[...]
        embed_ref[pl.ds(half - at, half)] = back_ref[...]
        d_inner = nt_dot(embed_ref[...].astype(jnp.bfloat16), mix_ref[...])
        d_pre = (d_inner * slope_ref[...]).astype(jnp.bfloat16)
        pre_ref[...] = d_pre
        ends[0][...] = d_pre[:step]
        ends[1][...] = d_pre[bins - step :]

    end = jax.ShapeDtypeStruct((step, inner), jnp.bfloat16)
    return pl.pallas_call(
        kernel,
        out_shape=(
            jax.ShapeDtypeStruct((bins, width), jnp.float32),
            jax.ShapeDtypeStruct((bins, inner), jnp.bfloat16),
            end,
            end,
        ),
        in_specs=[pl.BlockSpec(memory_space=pltpu.SMEM)] + [full] * 4,
        out_specs=(full,) * 4,
        compiler_params=room(10),
    )(core, kept, back, mix, slope)


def local_pass(d_pre, taps, step):
    bins = d_pre.shape[0]
    width = taps.shape[1]
    full = pl.BlockSpec(memory_space=pltpu.VMEM)

    def kernel(pre_ref, taps_ref, out_ref):
        out_ref[...] = nt_dot(pre_ref[...], taps_ref[1])
        out_ref[: bins - step] += nt_dot(pre_ref[step:], taps_ref[0])
        out_ref[step:] += nt_dot(pre_ref[: bins - step], taps_ref[2])

    return pl.pallas_call(
        kernel,
        out_shape=jax.ShapeDtypeStruct((bins, width), jnp.float32),
        in_specs=[full] * 2,
        out_specs=full,
        compiler_params=room(12),
    )(d_pre, taps)


def last_pass(before, after, d_act, taps, factor, xhat, inverse, d_embed):
    step = before.shape[0]
    bins, width = d_act.shape
    full = pl.BlockSpec(memory_space=pltpu.VMEM)

    def kernel(before_ref, after_ref, act_ref, first_ref, last_ref, *rest):
        factor_ref, xhat_ref, inverse_ref, embed_ref, out_ref = rest
        head = nt_dot(before_ref[...], last_ref[0])
        tail = nt_dot(after_ref[...], first_ref[0])
        for top in range(0, bins, step):
            at = pl.ds(top, step)
            d = act_ref[at]
            if top == 0:
                d = d + head
            if top == bins - step:
                d = d + tail
            d = d * factor_ref[at]
            xhat = xhat_ref[at]
            middle = jnp.mean(d, axis=1, keepdims=True)
            slant = jnp.mean(d * xhat, axis=1, keepdims=True)
            out_ref[at] = embed_ref[at] + inverse_ref[at] * (d - middle - xhat * slant)

    def tap(i):
        return pl.BlockSpec((1,) + taps.shape[1:], lambda j: (i, 0, 0))

    return pl.pallas_call(
        kernel,
        out_shape=jax.ShapeDtypeStruct((bins, width), jnp.float32),
        grid=(1,),
        in_specs=[full] * 3 + [tap(0), tap(2)] + [full] * 4,
        out_specs=full,
        compiler_params=room(16),
    )(before, after, d_act, taps, taps, factor, xhat, inverse, d_embed)


def shards(
    inputs,
    layernorm_gain,
    dilated_weight,
    mix_weight,
    head_weight,
    head_bias,
    stored_tiles,
    slot_tiles,
):
    n_q = lax.axis_size(SEQ)
    n_x = lax.axis_size("x")
    n_c = lax.axis_size("core")
    x_index = lax.axis_index("x")
    core = lax.axis_index("core")
    bins, width = inputs.shape[1:]
    half = bins // n_c
    tracks = head_weight.shape[1] * n_x * n_c
    slots, _, tile = stored_tiles.shape
    spans = tracks // tile
    depth = n_q * n_c * slots
    want = n_c * spans
    own_tracks = head_weight.shape[1]
    own_spans = own_tracks // tile

    def step(value, shift):
        return lax.ppermute(value, "x", [(i, (i + shift) % n_x) for i in range(n_x)])

    before, after = halo(inputs[0, bins - DILATION_STEP :], inputs[0, :DILATION_STEP])
    block = head_block(head_weight, head_bias, 16)
    outbound = gate(arrange(stored_tiles, n_q * n_c, (block,)), before, after)
    pieces = lax.all_to_all(
        outbound.reshape(depth, half, tile), ("z", "y", "core"), 0, 0, tiled=True
    )
    near = [step(block, 1), step(block, -1)]
    block_x = (x_index + jnp.array([0, 0, -1, -1, 1, 1, 2, 2], jnp.int32)) % n_x
    block_c = (core + jnp.array([0, 1, 0, 1, 0, 1, 0, 1], jnp.int32)) % n_c
    group_of = block_x * n_c + block_c

    table = slot_tiles.reshape(n_q, n_x, n_c * slots).transpose(1, 0, 2).reshape(n_x, depth)
    dest = jnp.where(table >= 0, table // want, n_x)
    chips = jnp.arange(n_x, dtype=jnp.int32)
    marks = dest[:, :, None] == chips[None, None, :]
    place = jnp.arange(depth, dtype=jnp.int32)
    same = dest[:, :, None] == dest[:, None, :]
    rank = jnp.sum(same & (place[None, None, :] < place[None, :, None]), axis=2, dtype=jnp.int32)
    sizes = jnp.sum(marks, axis=1, dtype=jnp.int32)
    fullest = jnp.max(jnp.where(chips[:, None] == chips[None, :], 0, sizes))
    my_dest = lax.dynamic_index_in_dim(dest, x_index, 0, keepdims=False)
    my_rank = lax.dynamic_index_in_dim(rank, x_index, 0, keepdims=False)
    shifted = (my_dest - x_index) % n_x
    shifted = jnp.where(my_dest < n_x, shifted, n_x)
    order = jnp.arange(want, dtype=jnp.int32)
    hit = (shifted[None, None, :] == chips[:, None, None]) & (
        my_rank[None, None, :] == order[None, :, None]
    )
    outgoing = jnp.sum(hit * place, axis=2, dtype=jnp.int32)

    spots = jnp.arange(want, dtype=jnp.int32)
    spot_side = spots // own_spans % n_c
    spot_span = (
        jnp.repeat(group_of, n_c * own_spans, total_repeat_length=want) * own_spans
        + spots % own_spans
    )
    tiles_wanted = (x_index * n_c + (core + spot_side) % n_c) * spans + spot_span
    turn = ((x_index - chips) % n_x)[:, None]
    spill = want - ROOM
    usual = want + (turn - 1) * ROOM + rank
    rare = want + (n_x - 1) * ROOM + (turn - 1) * spill + rank - ROOM
    spot_in = jnp.where(turn == 0, rank, jnp.where(rank < ROOM, usual, rare))
    found = tiles_wanted[:, None, None] == table[None]
    plan = jnp.sum(found * spot_in[None], axis=(1, 2), dtype=jnp.int32)
    plan = jnp.concatenate([plan, (fullest > ROOM).astype(jnp.int32)[None]])

    core_at = core.astype(jnp.int32)[None]
    act, xhat, factor, scale = norm_pass(before, inputs[0], after, layernorm_gain)
    cut = own_tracks // 2
    far = [
        step(gate(near[0][:cut], plan, scale), 1),
        step(gate(near[1][cut:], plan, scale), -1),
    ]
    slope, mine, theirs, mark = forward_pass(
        core_at, act, inputs[0], dilated_weight, mix_weight, half
    )
    blocks = []
    for parts in ([block], [near[0]], [near[1]]):
        blocks += [parts, [core_swap(part) for part in parts]]
    blocks += [far, [core_swap(gate(part, mark)) for part in far]]
    other = core_swap(theirs)

    outgoing = gate(outgoing, plan, other, *blocks[-1], lead=LEAD)
    picked = {d: pick(pieces, outgoing[d, :ROOM])[0] for d in (2, 1, 3)}
    sent = {d: step(picked[d], d) for d in (2, 1, 3)}
    arrived = [sent[d] for d in range(1, n_x)]

    def extra(first, last):
        def send(pieces, outgoing):
            out = []
            for d in range(1, n_x):
                v = step(pick(pieces, outgoing[d, first:last])[0], d)
                out.append(jnp.pad(v, ((0, want - last), (0, 0), (0, 0))))
            return tuple(out)

        return send

    def roomy(pieces, outgoing):
        shape = (want - ROOM,) + pieces.shape[1:]
        return tuple(blank(shape, pieces.dtype) for _ in range(n_x - 1))

    level = (fullest > ROOM).astype(jnp.int32) + (fullest > ROOM + SPARE)
    more = lax.switch(
        level,
        [roomy, extra(ROOM, ROOM + SPARE), extra(ROOM, want)],
        pieces,
        outgoing,
    )
    local, _ = pick(pieces, outgoing[0])
    sig, ratio, full_head = head_pass(mine, other, blocks, own_tracks, [local] + list(more))
    d_mine, d_theirs = grad_pass(plan, sig, ratio, [local] + arrived + list(more), own_spans)
    leaving = jnp.dot(d_theirs, full_head, preferred_element_type=jnp.float32)
    kept = jnp.dot(d_mine, full_head, preferred_element_type=jnp.float32)
    d_embed, d_pre, first, last = inner_pass(
        core_at, kept, core_swap(leaving), mix_weight, slope, DILATION_STEP
    )
    before, after = halo(last, first)
    d_act = local_pass(d_pre, dilated_weight, DILATION_STEP)
    grad = last_pass(before, after, d_act, dilated_weight, factor, xhat, scale, d_embed)
    return grad[None]


def solution(mesh):
    chips = jax.sharding.Mesh(
        np.asarray(mesh.devices).reshape(4, 4, 4, 2), ("z", "y", "x", "core")
    )
    in_specs = (
        P(TRK, SEQ, None),
        P(),
        P(),
        P(),
        P(None, TRK),
        P(TRK),
        P(SEQ + TRK, None, None),
        P(),
    )
    out_specs = P(TRK, SEQ, None)
    return jax.shard_map(
        shards, mesh=chips, in_specs=in_specs, out_specs=out_specs, check_vma=False
    )
```

time: 189 us -> 145 us (0.77)
  Pallas kernels: 0 us -> 39.9 us
  matrix products: 35.8 us -> 3.6 us
  blocking collectives: 26.7 us -> 0 us
  between operations: 14.4 us -> 1.99 us
  starting transfers between devices: 29.8 us -> 37.6 us
  waiting for transfers between devices: 37.1 us -> 29.9 us
  local copies, waits for them, and re-layouts: 30.8 us -> 23.7 us
  other arithmetic: 12 us -> 7.25 us
    pallas_call x0 -> x22, Pallas kernels: none -> 39.9 us  [the longest x1 12.2 us: head_pass(): pl.pallas_call(lambda *refs: head_kernel(counts, own, *refs), out_shape=(...]
    dot_general x9 -> x2, matrix products: 35.8 us -> 3.6 us  [the longest x1 1.8 us: shards(): kept = jnp.dot(d_mine, full_head, preferred_element_type=jnp.float32)]
    all_to_all x2 -> x1, waiting for transfers between devices: 29.7 us -> 1.77 us  [shards(): lax.all_to_all(outbound.reshape(depth, half, tile), ('z', 'y', 'core'), 0...]
    all_gather x1 -> x0, blocking collectives: 26.7 us -> none  [shards(): full_bias = lax.all_gather(head_bias, TRK, axis=0, tiled=True)]
    ppermute x4 -> x11, waiting for transfers between devices: 4.28 us -> 26.1 us  [the longest x7 21.6 us: step(): lax.ppermute(value, 'x', [(i, (i + shift) % n_x) for i in range(n_x)])]
    unnamed x28 -> x88, local copies, waits for them, and re-layouts: 2.07 us -> 18.4 us
    ppermute x4 -> x11, starting transfers between devices: 14.5 us -> 26.9 us  [the longest x4 15.2 us: halo(): return (lax.ppermute(last, SEQ, up), lax.ppermute(first, SEQ, down))]
    gather x2 -> x1, local copies, waits for them, and re-layouts: 9.14 us -> 0.68 us  [shards(): jnp.repeat(group_of, n_c * own_spans, total_repeat_length=want) * own_spans]
  transfers between devices with their start and end apart: 9 -> 19, of which waited for: 3 -> 9; matrix products, arithmetic and copies ran while one was open for 26% -> 13% of each run, Pallas kernels for 0% -> 24%
where the time goes in v2:
time: 145 us; the launch traced here: 144 us
  Pallas kernels  39.9 us (28%)
  starting transfers between devices  37.6 us (26%)
  waiting for transfers between devices  29.9 us (21%)
  local copies, waits for them, and re-layouts  23.7 us (16%)
  other arithmetic  7.25 us (5%)
  matrix products  3.6 us (2%)
  between operations  1.99 us (1%)
    ppermute x7, waiting for transfers between devices, step(): lax.ppermute(value, 'x', [(i, (i + shift) % n_x) for i in range(n_x)])  21.6 us
    unnamed x88, local copies, waits for them, and re-layouts  18.4 us
    ppermute x4, starting transfers between devices, halo(): return (lax.ppermute(last, SEQ, up), lax.ppermute(first, SEQ, down))  15.2 us
    pallas_call x1, Pallas kernels, head_pass(): pl.pallas_call(lambda *refs: head_kernel(counts, own, *refs), out_shape=(...  12.2 us
    ppermute x7, starting transfers between devices, step(): lax.ppermute(value, 'x', [(i, (i + shift) % n_x) for i in range(n_x)])  11.7 us
    pallas_call x4, Pallas kernels, pick(): pl.pallas_call(lambda *refs: pick_kernel(count, *refs), out_shape=(jax.Sh...  10.7 us
    all_to_all x1, starting transfers between devices, shards(): lax.all_to_all(outbound.reshape(depth, half, tile), ('z', 'y', 'core'), 0...  7.73 us
    add x1, other arithmetic, shards(): (x_index * n_c + (core + spot_side) % n_c) * spans + spot_span  5.01 us
  transfers between devices with their start and end apart: 19, of which 9 were waited for; matrix products, arithmetic and copies ran while one was open for 13% of the time, Pallas kernels for 24%

profile of v2, /device:TPU:56, one launch (start us, length us, event | category | flops | bytes accessed | tf_op | source)
XLA Modules:
  0.0 143.9 jit_solution(296205995906839169)
XLA Ops:
  2.6 2.8 %collective-permute-start.12 = (bf16[528,1536]{1,0:T(8,128)(2,1)S(1)}, bf16[528,1536]{1,0:T(8,128)(2,1)}, u32[]{:S(2)}, u32[]{:S(2)}) collective-permute-start(bf16[528,1536]{1,0:T(8,128)(2,1)S(1)} %shard_map.102.rest_0_.refs_2_), channel_id=1, source_target_pairs={{0,6},{2,0},{4,2},{6,4},{1,7},{3,1},{5,3},{7,5},{8,14},{10,8},{12,... | collective-permute-start | bytes 4866056 | tf_op jit(solution)/shard_map/ppermute | solution.py:480
  5.5 2.7 %collective-permute-start.7 = (bf16[64,1536]{1,0:T(8,128)(2,1)S(1)}, bf16[64,1536]{1,0:T(8,128)(2,1)S(1)}, u32[]{:S(2)}, u32[]{:S(2)}) collective-permute-start(bf16[64,1536]{1,0:T(8,128)(2,1)S(1)} %get-tuple-element.89), channel_id=1, source_target_pairs={{8,0},{16,8},{24,16},{32,24},{40,32},{48,40},{56,48},{64,56},{72,6... | collective-permute-start | bytes 589832 | tf_op jit(solution)/shard_map/ppermute | solution.py:25
  8.2 5.3 %collective-permute-start.6 = (bf16[64,1536]{1,0:T(8,128)(2,1)S(1)}, bf16[64,1536]{1,0:T(8,128)(2,1)S(1)}, u32[]{:S(2)}, u32[]{:S(2)}) collective-permute-start(bf16[64,1536]{1,0:T(8,128)(2,1)S(1)} %get-tuple-element.90), channel_id=1, source_target_pairs={{0,8},{8,16},{16,24},{24,32},{32,40},{40,48},{48,56},{56,64},{64,7... | collective-permute-start | bytes 589832 | tf_op jit(solution)/shard_map/ppermute | solution.py:25
  13.9 3.3 %shard_map.108.refs_0_ = bf16[32,4,128,128]{3,2,1,0:T(8,128)(2,1)} custom-call(bf16[4,32,128,128]{3,2,1,0:T(8,128)(2,1)} %bitcast.56, bf16[528,1536]{1,0:T(8,128)(2,1)} %copy-done.1), custom_call_target="tpu_custom_call" | custom-call | tf_op jit(solution)/shard_map/pallas_call | solution.py:62
  19.4 7.7 %all-to-all-start = ((bf16[128,128,128]{2,1,0:T(8,128)(2,1)}), bf16[128,128,128]{2,1,0:T(8,128)(2,1)}, u32[]{:S(2)}, u32[]{:S(2)}) async-start(bf16[128,128,128]{2,1,0:T(8,128)(2,1)} %bitcast.55), calls=%async_computation | async-start | bytes 8388608 | tf_op jit(solution)/shard_map/all_to_all | solution.py:485
  28.9 5.0 %fusion.4 = s32[64]{0:T(128)S(1)} fusion(pred[64]{0:T(512)(128)(4,1)S(1)} %copy-done.41, pred[64]{0:T(512)(128)(4,1)S(1)} %copy-done.40, pred[64]{0:T(512)(128)(4,1)S(1)} %copy-done.39, pred[64]{0:T(512)(128)(4,1)S(1)} %copy-done.38, pred[64]{0:T(512)(128)(4,1)S(1)} %copy-done.37, pred[64]{0:T(512)(128)(4,1)S(1)} %copy-done.36, ...), kind=kLoop, calls=%fused_computation.52 | loop fusion | flops 3008 | bytes 744 | tf_op jit(solution)/shard_map/add | solution.py:518
  40.2 2.2 %slice.73.refs_0_ = bf16[272,1536]{1,0:T(8,128)(2,1)} slice(bf16[528,1536]{1,0:T(8,128)(2,1)} %collective-permute-done.12.refs_6_), slice={[256:528], [0:1536]} | slice | bytes 1671168 | tf_op jit(solution)/shard_map/slice | solution.py:533
  42.3 3.8 %collective-permute-start.15 = (bf16[272,1536]{1,0:T(8,128)(2,1)}, bf16[272,1536]{1,0:T(8,128)(2,1)}, u32[]{:S(2)}, u32[]{:S(2)}) collective-permute-start(bf16[272,1536]{1,0:T(8,128)(2,1)} %shard_map.104), channel_id=1, source_target_pairs={{0,6},{2,0},{4,2},{6,4},{1,7},{3,1},{5,3},{7,5},{8,14},{10,8},{12,... | collective-permute-start | bytes 2506760 | tf_op jit(solution)/shard_map/ppermute | solution.py:480
  46.1 2.2 %slice.72.refs_0_ = bf16[256,1536]{1,0:T(8,128)(2,1)} slice(bf16[528,1536]{1,0:T(8,128)(2,1)} %collective-permute-done.10.refs_4_), slice={[0:256], [0:1536]} | slice | bytes 1572864 | tf_op jit(solution)/shard_map/slice | solution.py:532
  48.4 3.0 %copy-done = bf16[3,1536,768]{2,1,0:T(8,128)(2,1)S(1)} copy-done((bf16[3,1536,768]{2,1,0:T(8,128)(2,1)S(1)}, bf16[3,1536,768]{2,1,0:T(8,128)(2,1)}, u32[]{:S(2)}) %copy-start) | copy-done | bytes 7077912
  52.7 3.9 %shard_map.101 = (f32[256,768]{1,0:T(8,128)S(1)}, bf16[128,1536]{1,0:T(8,128)(2,1)S(1)}, bf16[128,1536]{1,0:T(8,128)(2,1)S(1)}, f32[8,128]{1,0:T(8,128)S(1)}) custom-call(s32[1]{0:T(128)} %bitcast.6.core_ref, bf16[384,1536]{1,0:T(8,128)(2,1)S(1)} %copy-done.14, bf16[256,1536]{1,0:T(8,128)(2,1)S(1)} %bitcast.53, bf16[3,1536,768]{2,1,0:T(8,128)(2,1)S(1)} %copy-done, ...), custom_call_target="tpu_custom_call" | custom-call | tf_op jit(solution)/shard_map/pallas_call | solution.py:249
  59.5 4.2 %collective-permute-done.15.refs_9_ = bf16[272,1536]{1,0:T(8,128)(2,1)} collective-permute-done((bf16[272,1536]{1,0:T(8,128)(2,1)}, bf16[272,1536]{1,0:T(8,128)(2,1)}, u32[]{:S(2)}, u32[]{:S(2)}) %collective-permute-start.15) | collective-permute-done | bytes 835616 | tf_op jit(solution)/shard_map/ppermute | solution.py:480
  63.7 2.1 %copy.22.refs_0_ = bf16[272,1536]{1,0:T(8,128)(2,1)} copy(bf16[272,1536]{1,0:T(8,128)(2,1)} %collective-permute-done.15.refs_9_) | data formatting | bytes 1671168
  77.1 2.3 %shard_map.112 = (bf16[24,128,128]{2,1,0:T(8,128)(2,1)S(1)}, f32[8,128]{1,0:T(8,128)}) custom-call(s32[24]{0:T(128)S(1)} %get-tuple-element.93.refs_0_, bf16[128,128,128]{2,1,0:T(8,128)(2,1)} %all-to-all-done.refs_1_), custom_call_target="tpu_custom_call" | custom-call | tf_op jit(solution)/shard_map/pallas_call | solution.py:160
  80.1 2.4 %shard_map.113 = (bf16[24,128,128]{2,1,0:T(8,128)(2,1)S(1)}, f32[8,128]{1,0:T(8,128)}) custom-call(s32[24]{0:T(128)S(1)} %get-tuple-element.92.refs_0_, bf16[128,128,128]{2,1,0:T(8,128)(2,1)} %all-to-all-done.refs_1_), custom_call_target="tpu_custom_call" | custom-call | tf_op jit(solution)/shard_map/pallas_call | solution.py:160
  82.5 3.8 %collective-permute-start.19 = (bf16[24,128,128]{2,1,0:T(8,128)(2,1)S(1)}, bf16[24,128,128]{2,1,0:T(8,128)(2,1)S(1)}, u32[]{:S(2)}, u32[]{:S(2)}) collective-permute-start(bf16[24,128,128]{2,1,0:T(8,128)(2,1)S(1)} %get-tuple-element.71), channel_id=1, source_target_pairs={{0,4},{2,6},{4,0},{6,2},{1,5},{3,7},{5,1},{7,3},{8,12},{10,14},{12... | collective-permute-start | bytes 2359304 | tf_op jit(solution)/shard_map/ppermute | solution.py:480
  86.4 2.3 %shard_map.114 = (bf16[24,128,128]{2,1,0:T(8,128)(2,1)S(1)}, f32[8,128]{1,0:T(8,128)}) custom-call(s32[24]{0:T(128)S(1)} %get-tuple-element.91.refs_0_, bf16[128,128,128]{2,1,0:T(8,128)(2,1)} %all-to-all-done.refs_1_), custom_call_target="tpu_custom_call" | custom-call | tf_op jit(solution)/shard_map/pallas_call | solution.py:160
  89.2 3.6 %shard_map.110 = (bf16[64,128,128]{2,1,0:T(8,128)(2,1)S(1)}, f32[8,128]{1,0:T(8,128)}) custom-call(s32[64]{0:T(128)S(1)} %slice_bitcast_fusion.11.refs_0_, bf16[128,128,128]{2,1,0:T(8,128)(2,1)} %all-to-all-done.refs_1_), custom_call_target="tpu_custom_call" | custom-call | tf_op jit(solution)/shard_map/pallas_call | solution.py:160
  93.0 12.2 %shard_map.111 = (f32[256,4096]{1,0:T(8,128)S(1)}, f32[256,4096]{1,0:T(8,128)S(1)}, bf16[4096,1536]{1,0:T(8,128)(2,1)S(1)}) custom-call(bf16[128,1536]{1,0:T(8,128)(2,1)S(1)} %copy-done.22, bf16[128,1536]{1,0:T(8,128)(2,1)} %collective-permute-done.8.refs_2_.refs_1_, bf16[528,1536]{1,0:T(8,128)(2,1)S(1)} %copy-done.2, ...), custom_call_target="tpu_custom_call" | custom-call | tf_op jit(solution)/shard_map/pallas_call | solution.py:300
  105.2 13.2 %collective-permute-done.19.refs_5_ = bf16[24,128,128]{2,1,0:T(8,128)(2,1)S(1)} collective-permute-done((bf16[24,128,128]{2,1,0:T(8,128)(2,1)S(1)}, bf16[24,128,128]{2,1,0:T(8,128)(2,1)S(1)}, u32[]{:S(2)}, u32[]{:S(2)}) %collective-permute-start.19) | collective-permute-done | bytes 786464 | tf_op jit(solution)/shard_map/ppermute | solution.py:480
  126.8 5.3 %collective-permute-start.22 = (bf16[64,768]{1,0:T(8,128)(2,1)S(1)}, bf16[64,768]{1,0:T(8,128)(2,1)S(1)}, u32[]{:S(2)}, u32[]{:S(2)}) collective-permute-start(bf16[64,768]{1,0:T(8,128)(2,1)S(1)} %get-tuple-element.77), channel_id=1, source_target_pairs={{0,8},{8,16},{16,24},{24,32},{32,40},{40,48},{48,56},{56,64},{64,7... | collective-permute-start | bytes 294920 | tf_op jit(solution)/shard_map/ppermute | solution.py:25
  134.1 2.3 %shard_map.117.act_ref = f32[256,1536]{1,0:T(8,128)S(1)} custom-call(bf16[256,768]{1,0:T(8,128)(2,1)S(1)} %get-tuple-element.79.pre_ref, bf16[3,1536,768]{2,1,0:T(8,128)(2,1)S(1)} %bitcast.51), custom_call_target="tpu_custom_call" | custom-call | tf_op jit(solution)/shard_map/pallas_call | solution.py:410
  136.4 4.5 %collective-permute-done.23.after_ref = bf16[64,768]{1,0:T(8,128)(2,1)S(1)} collective-permute-done((bf16[64,768]{1,0:T(8,128)(2,1)S(1)}, bf16[64,768]{1,0:T(8,128)(2,1)S(1)}, u32[]{:S(2)}, u32[]{:S(2)}) %collective-permute-start.23) | collective-permute-done | bytes 98336 | tf_op jit(solution)/shard_map/ppermute | solution.py:25
  140.9 3.0 %shard_map.118 = f32[256,1536]{1,0:T(8,128)} custom-call(bf16[64,768]{1,0:T(8,128)(2,1)S(1)} %collective-permute-done.22.before_ref, bf16[64,768]{1,0:T(8,128)(2,1)S(1)} %collective-permute-done.23.after_ref, f32[256,1536]{1,0:T(8,128)S(1)} %shard_map.117.act_ref, bf16[3,1536,768]{2,1,0:T(8,128)(2,1)S(1)} %bitcast.51, bf16[3,1536,768]{2,1,0:T(8,128)(2,1)S(1)} %bitcast.51, ...), custom_call_target="tpu_custom_call" | custom-call | tf_op jit(solution)/shard_map/pallas_call | solution.py:444
  (155 shorter events, 38.7 us)
Async XLA Ops:
  2.2 11.3 %copy-start.34 = (s32[512]{0:T(512)S(1)}, s32[512]{0:T(512)}, u32[]{:S(2)}) copy-start(s32[512]{0:T(512)} %param.22) | copy-start | bytes 6148
  2.6 11.2 %copy-start.1 = (bf16[528,1536]{1,0:T(8,128)(2,1)}, bf16[528,1536]{1,0:T(8,128)(2,1)S(1)}, u32[]{:S(2)}) copy-start(bf16[528,1536]{1,0:T(8,128)(2,1)S(1)} %shard_map.102.rest_0_.refs_2_) | copy-start | bytes 4866052
  2.6 37.5 %collective-permute-start.12 = (bf16[528,1536]{1,0:T(8,128)(2,1)S(1)}, bf16[528,1536]{1,0:T(8,128)(2,1)}, u32[]{:S(2)}, u32[]{:S(2)}) collective-permute-start(bf16[528,1536]{1,0:T(8,128)(2,1)S(1)} %shard_map.102.rest_0_.refs_2_), channel_id=1, source_target_pairs={{0,6},{2,0},{4,2},{6,4},{1,7},{3,1},{5,3},{7,5},{8,14},{10,8},{12,... | collective-permute-start | bytes 4866056 | tf_op jit(solution)/shard_map/ppermute | solution.py:480
  5.5 40.7 %collective-permute-start.10 = (bf16[528,1536]{1,0:T(8,128)(2,1)S(1)}, bf16[528,1536]{1,0:T(8,128)(2,1)}, u32[]{:S(2)}, u32[]{:S(2)}) collective-permute-start(bf16[528,1536]{1,0:T(8,128)(2,1)S(1)} %shard_map.102.rest_0_.refs_2_), channel_id=1, source_target_pairs={{0,2},{2,4},{4,6},{6,0},{1,3},{3,5},{5,7},{7,1},{8,10},{10,12},{12... | collective-permute-start | bytes 4866056 | tf_op jit(solution)/shard_map/ppermute | solution.py:480
  5.5 12.4 %collective-permute-start.7 = (bf16[64,1536]{1,0:T(8,128)(2,1)S(1)}, bf16[64,1536]{1,0:T(8,128)(2,1)S(1)}, u32[]{:S(2)}, u32[]{:S(2)}) collective-permute-start(bf16[64,1536]{1,0:T(8,128)(2,1)S(1)} %get-tuple-element.89), channel_id=1, source_target_pairs={{8,0},{16,8},{24,16},{32,24},{40,32},{48,40},{56,48},{64,56},{72,6... | collective-permute-start | bytes 589832 | tf_op jit(solution)/shard_map/ppermute | solution.py:25
  8.2 9.8 %collective-permute-start.6 = (bf16[64,1536]{1,0:T(8,128)(2,1)S(1)}, bf16[64,1536]{1,0:T(8,128)(2,1)S(1)}, u32[]{:S(2)}, u32[]{:S(2)}) collective-permute-start(bf16[64,1536]{1,0:T(8,128)(2,1)S(1)} %get-tuple-element.90), channel_id=1, source_target_pairs={{0,8},{8,16},{16,24},{24,32},{32,40},{40,48},{48,56},{56,64},{64,7... | collective-permute-start | bytes 589832 | tf_op jit(solution)/shard_map/ppermute | solution.py:25
  19.4 15.5 %copy-start.18 = (bf16[64,1536]{1,0:T(8,128)(2,1)S(1)}, bf16[64,1536]{1,0:T(8,128)(2,1)}, u32[]{:S(2)}) copy-start(bf16[64,1536]{1,0:T(8,128)(2,1)} %copy-done.17) | copy-start | bytes 589828
  19.4 15.5 %copy-start.20 = (bf16[64,1536]{1,0:T(8,128)(2,1)S(1)}, bf16[64,1536]{1,0:T(8,128)(2,1)}, u32[]{:S(2)}) copy-start(bf16[64,1536]{1,0:T(8,128)(2,1)} %copy-done.19) | copy-start | bytes 589828
  19.4 56.0 %all-to-all-start = ((bf16[128,128,128]{2,1,0:T(8,128)(2,1)}), bf16[128,128,128]{2,1,0:T(8,128)(2,1)}, u32[]{:S(2)}, u32[]{:S(2)}) async-start(bf16[128,128,128]{2,1,0:T(8,128)(2,1)} %bitcast.55), calls=%async_computation | async-start | bytes 8388608 | tf_op jit(solution)/shard_map/all_to_all | solution.py:485
  42.3 21.4 %collective-permute-start.15 = (bf16[272,1536]{1,0:T(8,128)(2,1)}, bf16[272,1536]{1,0:T(8,128)(2,1)}, u32[]{:S(2)}, u32[]{:S(2)}) collective-permute-start(bf16[272,1536]{1,0:T(8,128)(2,1)} %shard_map.104), channel_id=1, source_target_pairs={{0,6},{2,0},{4,2},{6,4},{1,7},{3,1},{5,3},{7,5},{8,14},{10,8},{12,... | collective-permute-start | bytes 2506760 | tf_op jit(solution)/shard_map/ppermute | solution.py:480
  48.4 19.9 %collective-permute-start.14 = (bf16[256,1536]{1,0:T(8,128)(2,1)}, bf16[256,1536]{1,0:T(8,128)(2,1)}, u32[]{:S(2)}, u32[]{:S(2)}) collective-permute-start(bf16[256,1536]{1,0:T(8,128)(2,1)} %shard_map.103), channel_id=1, source_target_pairs={{0,2},{2,4},{4,6},{6,0},{1,3},{3,5},{5,7},{7,1},{8,10},{10,12},{12... | collective-permute-start | bytes 2359304 | tf_op jit(solution)/shard_map/ppermute | solution.py:480
  65.8 7.7 %collective-permute-start.17 = (bf16[272,1536]{1,0:T(8,128)(2,1)}, bf16[272,1536]{1,0:T(8,128)(2,1)}, u32[]{:S(2)}, u32[]{:S(2)}) collective-permute-start(bf16[272,1536]{1,0:T(8,128)(2,1)} %shard_map.106), channel_id=1, source_target_pairs={{0,1},{1,0},{2,3},{3,2},{4,5},{5,4},{6,7},{7,6},{8,9},{9,8},{10,11... | collective-permute-start | bytes 2506760 | tf_op jit(solution)/shard_map/ppermute | solution.py:29
  65.8 22.9 %collective-permute-start.9 = (bf16[528,1536]{1,0:T(8,128)(2,1)S(1)}, bf16[528,1536]{1,0:T(8,128)(2,1)S(1)}, u32[]{:S(2)}, u32[]{:S(2)}) collective-permute-start(bf16[528,1536]{1,0:T(8,128)(2,1)S(1)} %copy-done.2), channel_id=1, source_target_pairs={{0,1},{1,0},{2,3},{3,2},{4,5},{5,4},{6,7},{7,6},{8,9},{9,8},{10,11... | collective-permute-start | bytes 4866056 | tf_op jit(solution)/shard_map/ppermute | solution.py:29
  70.4 3.2 %collective-permute-start.16 = (bf16[256,1536]{1,0:T(8,128)(2,1)}, bf16[256,1536]{1,0:T(8,128)(2,1)}, u32[]{:S(2)}, u32[]{:S(2)}) collective-permute-start(bf16[256,1536]{1,0:T(8,128)(2,1)} %shard_map.105), channel_id=1, source_target_pairs={{0,1},{1,0},{2,3},{3,2},{4,5},{5,4},{6,7},{7,6},{8,9},{9,8},{10,11... | collective-permute-start | bytes 2359304 | tf_op jit(solution)/shard_map/ppermute | solution.py:29
  70.4 3.2 %collective-permute-start.8 = (bf16[128,1536]{1,0:T(8,128)(2,1)}, bf16[128,1536]{1,0:T(8,128)(2,1)}, u32[]{:S(2)}, u32[]{:S(2)}) collective-permute-start(bf16[128,1536]{1,0:T(8,128)(2,1)} %copy-done.26), channel_id=1, source_target_pairs={{0,1},{1,0},{2,3},{3,2},{4,5},{5,4},{6,7},{7,6},{8,9},{9,8},{10,11... | collective-permute-start | bytes 1179656 | tf_op jit(solution)/shard_map/ppermute | solution.py:29
  71.9 21.0 %collective-permute-start.13 = (bf16[528,1536]{1,0:T(8,128)(2,1)}, bf16[528,1536]{1,0:T(8,128)(2,1)}, u32[]{:S(2)}, u32[]{:S(2)}) collective-permute-start(bf16[528,1536]{1,0:T(8,128)(2,1)} %collective-permute-done.12.refs_6_), channel_id=1, source_target_pairs={{0,1},{1,0},{2,3},{3,2},{4,5},{5,4},{6,7},{7,6},{8,9},{9,8},{10,11... | collective-permute-start | bytes 4866056 | tf_op jit(solution)/shard_map/ppermute | solution.py:29
  75.4 17.5 %collective-permute-start.11 = (bf16[528,1536]{1,0:T(8,128)(2,1)}, bf16[528,1536]{1,0:T(8,128)(2,1)S(1)}, u32[]{:S(2)}, u32[]{:S(2)}) collective-permute-start(bf16[528,1536]{1,0:T(8,128)(2,1)} %collective-permute-done.10.refs_4_), channel_id=1, source_target_pairs={{0,1},{1,0},{2,3},{3,2},{4,5},{5,4},{6,7},{7,6},{8,9},{9,8},{10,11... | collective-permute-start | bytes 4866056 | tf_op jit(solution)/shard_map/ppermute | solution.py:29
  79.4 25.7 %collective-permute-start.18 = (bf16[24,128,128]{2,1,0:T(8,128)(2,1)S(1)}, bf16[24,128,128]{2,1,0:T(8,128)(2,1)S(1)}, u32[]{:S(2)}, u32[]{:S(2)}) collective-permute-start(bf16[24,128,128]{2,1,0:T(8,128)(2,1)S(1)} %get-tuple-element.70), channel_id=1, source_target_pairs={{0,2},{2,4},{4,6},{6,0},{1,3},{3,5},{5,7},{7,1},{8,10},{10,12},{12... | collective-permute-start | bytes 2359304 | tf_op jit(solution)/shard_map/ppermute | solution.py:480
  82.5 35.8 %collective-permute-start.19 = (bf16[24,128,128]{2,1,0:T(8,128)(2,1)S(1)}, bf16[24,128,128]{2,1,0:T(8,128)(2,1)S(1)}, u32[]{:S(2)}, u32[]{:S(2)}) collective-permute-start(bf16[24,128,128]{2,1,0:T(8,128)(2,1)S(1)} %get-tuple-element.71), channel_id=1, source_target_pairs={{0,4},{2,6},{4,0},{6,2},{1,5},{3,7},{5,1},{7,3},{8,12},{10,14},{12... | collective-permute-start | bytes 2359304 | tf_op jit(solution)/shard_map/ppermute | solution.py:480
  88.7 31.4 %collective-permute-start.20 = (bf16[24,128,128]{2,1,0:T(8,128)(2,1)S(1)}, bf16[24,128,128]{2,1,0:T(8,128)(2,1)S(1)}, u32[]{:S(2)}, u32[]{:S(2)}) collective-permute-start(bf16[24,128,128]{2,1,0:T(8,128)(2,1)S(1)} %get-tuple-element.72), channel_id=1, source_target_pairs={{0,6},{2,0},{4,2},{6,4},{1,7},{3,1},{5,3},{7,5},{8,14},{10,8},{12,... | collective-permute-start | bytes 2359304 | tf_op jit(solution)/shard_map/ppermute | solution.py:480
  92.9 27.2 %copy-start.24 = (s32[65]{0:T(128)S(1)}, s32[65]{0:T(128)}, u32[]{:S(2)}) copy-start(s32[65]{0:T(128)} %pad_add_fusion.refs_1_.refs_0_) | copy-start | bytes 784
  123.6 2.4 %collective-permute-start.21 = (f32[128,1536]{1,0:T(8,128)S(1)}, f32[128,1536]{1,0:T(8,128)S(1)}, u32[]{:S(2)}, u32[]{:S(2)}) collective-permute-start(f32[128,1536]{1,0:T(8,128)S(1)} %fusion.18), channel_id=1, source_target_pairs={{0,1},{1,0},{2,3},{3,2},{4,5},{5,4},{6,7},{7,6},{8,9},{9,8},{10,11... | collective-permute-start | bytes 2359304 | tf_op jit(solution)/shard_map/ppermute | solution.py:29
  126.8 9.6 %collective-permute-start.22 = (bf16[64,768]{1,0:T(8,128)(2,1)S(1)}, bf16[64,768]{1,0:T(8,128)(2,1)S(1)}, u32[]{:S(2)}, u32[]{:S(2)}) collective-permute-start(bf16[64,768]{1,0:T(8,128)(2,1)S(1)} %get-tuple-element.77), channel_id=1, source_target_pairs={{0,8},{8,16},{16,24},{24,32},{32,40},{40,48},{48,56},{56,64},{64,7... | collective-permute-start | bytes 294920 | tf_op jit(solution)/shard_map/ppermute | solution.py:25
  132.2 8.8 %collective-permute-start.23 = (bf16[64,768]{1,0:T(8,128)(2,1)S(1)}, bf16[64,768]{1,0:T(8,128)(2,1)S(1)}, u32[]{:S(2)}, u32[]{:S(2)}) collective-permute-start(bf16[64,768]{1,0:T(8,128)(2,1)S(1)} %get-tuple-element.78), channel_id=1, source_target_pairs={{8,0},{16,8},{24,16},{32,24},{40,32},{48,40},{56,48},{64,56},{72,6... | collective-permute-start | bytes 294920 | tf_op jit(solution)/shard_map/ppermute | solution.py:25
  (38 other events, 185.9 us)

commit v3 on v2

--- a/solution.py
+++ b/solution.py
@@ -8,7 +8,7 @@
 
 DILATION_STEP = 64
 ROOM = 24
-SPARE = 8
+SPARE = 4
 LEAD = 12
 
 SQRT_HALF = 0.7071067811865476
@@ -149,7 +149,7 @@
         pltpu.make_async_copy(pieces_ref.at[index_ref[i]], out_ref.at[i], sem).start()
         return carry
 
-    lax.fori_loop(0, count, start, 0, unroll=8)
+    lax.fori_loop(0, count, start, 0, unroll=min(count, 8))
     mark_ref[...] = jnp.zeros_like(mark_ref)
     pltpu.make_async_copy(pieces_ref.at[pl.ds(0, count)], out_ref, sem).wait()
 

time: 145 us -> 145 us (level)
  no operation moved by 1% of the time
where the time goes in v3:
time: 145 us; the launch traced here: 144 us
  Pallas kernels  40.2 us (28%)
  starting transfers between devices  37.3 us (26%)
  waiting for transfers between devices  29.8 us (21%)
  local copies, waits for them, and re-layouts  23.7 us (16%)
  other arithmetic  7.25 us (5%)
  matrix products  3.6 us (2%)
  between operations  1.99 us (1%)
    ppermute x7, waiting for transfers between devices, step(): lax.ppermute(value, 'x', [(i, (i + shift) % n_x) for i in range(n_x)])  21.5 us
    unnamed x88, local copies, waits for them, and re-layouts  18.4 us
    ppermute x4, starting transfers between devices, halo(): return (lax.ppermute(last, SEQ, up), lax.ppermute(first, SEQ, down))  15.2 us
    pallas_call x1, Pallas kernels, head_pass(): pl.pallas_call(lambda *refs: head_kernel(counts, own, *refs), out_shape=(...  12.2 us
    ppermute x7, starting transfers between devices, step(): lax.ppermute(value, 'x', [(i, (i + shift) % n_x) for i in range(n_x)])  11.4 us
    pallas_call x4, Pallas kernels, pick(): pl.pallas_call(lambda *refs: pick_kernel(count, *refs), out_shape=(jax.Sh...  11 us
    all_to_all x1, starting transfers between devices, shards(): lax.all_to_all(outbound.reshape(depth, half, tile), ('z', 'y', 'core'), 0...  7.73 us
    add x1, other arithmetic, shards(): (x_index * n_c + (core + spot_side) % n_c) * spans + spot_span  5.01 us
  transfers between devices with their start and end apart: 19, of which 9 were waited for; matrix products, arithmetic and copies ran while one was open for 13% of the time, Pallas kernels for 24%

profile of v3, /device:TPU:56, one launch (start us, length us, event | category | flops | bytes accessed | tf_op | source)
XLA Modules:
  0.0 143.9 jit_solution(9212567181149970880)
XLA Ops:
  2.6 2.8 %collective-permute-start.12 = (bf16[528,1536]{1,0:T(8,128)(2,1)S(1)}, bf16[528,1536]{1,0:T(8,128)(2,1)}, u32[]{:S(2)}, u32[]{:S(2)}) collective-permute-start(bf16[528,1536]{1,0:T(8,128)(2,1)S(1)} %shard_map.102.rest_0_.refs_2_), channel_id=1, source_target_pairs={{0,6},{2,0},{4,2},{6,4},{1,7},{3,1},{5,3},{7,5},{8,14},{10,8},{12,... | collective-permute-start | bytes 4866056 | tf_op jit(solution)/shard_map/ppermute | solution.py:480
  5.5 2.7 %collective-permute-start.7 = (bf16[64,1536]{1,0:T(8,128)(2,1)S(1)}, bf16[64,1536]{1,0:T(8,128)(2,1)S(1)}, u32[]{:S(2)}, u32[]{:S(2)}) collective-permute-start(bf16[64,1536]{1,0:T(8,128)(2,1)S(1)} %get-tuple-element.89), channel_id=1, source_target_pairs={{8,0},{16,8},{24,16},{32,24},{40,32},{48,40},{56,48},{64,56},{72,6... | collective-permute-start | bytes 589832 | tf_op jit(solution)/shard_map/ppermute | solution.py:25
  8.2 5.3 %collective-permute-start.6 = (bf16[64,1536]{1,0:T(8,128)(2,1)S(1)}, bf16[64,1536]{1,0:T(8,128)(2,1)S(1)}, u32[]{:S(2)}, u32[]{:S(2)}) collective-permute-start(bf16[64,1536]{1,0:T(8,128)(2,1)S(1)} %get-tuple-element.90), channel_id=1, source_target_pairs={{0,8},{8,16},{16,24},{24,32},{32,40},{40,48},{48,56},{56,64},{64,7... | collective-permute-start | bytes 589832 | tf_op jit(solution)/shard_map/ppermute | solution.py:25
  13.9 3.3 %shard_map.108.refs_0_ = bf16[32,4,128,128]{3,2,1,0:T(8,128)(2,1)} custom-call(bf16[4,32,128,128]{3,2,1,0:T(8,128)(2,1)} %bitcast.56, bf16[528,1536]{1,0:T(8,128)(2,1)} %copy-done.1), custom_call_target="tpu_custom_call" | custom-call | tf_op jit(solution)/shard_map/pallas_call | solution.py:62
  19.4 7.7 %all-to-all-start = ((bf16[128,128,128]{2,1,0:T(8,128)(2,1)}), bf16[128,128,128]{2,1,0:T(8,128)(2,1)}, u32[]{:S(2)}, u32[]{:S(2)}) async-start(bf16[128,128,128]{2,1,0:T(8,128)(2,1)} %bitcast.55), calls=%async_computation | async-start | bytes 8388608 | tf_op jit(solution)/shard_map/all_to_all | solution.py:485
  28.9 5.0 %fusion.4 = s32[64]{0:T(128)S(1)} fusion(pred[64]{0:T(512)(128)(4,1)S(1)} %copy-done.41, pred[64]{0:T(512)(128)(4,1)S(1)} %copy-done.40, pred[64]{0:T(512)(128)(4,1)S(1)} %copy-done.39, pred[64]{0:T(512)(128)(4,1)S(1)} %copy-done.38, pred[64]{0:T(512)(128)(4,1)S(1)} %copy-done.37, pred[64]{0:T(512)(128)(4,1)S(1)} %copy-done.36, ...), kind=kLoop, calls=%fused_computation.52 | loop fusion | flops 3008 | bytes 744 | tf_op jit(solution)/shard_map/add | solution.py:518
  40.2 2.2 %slice.73.refs_0_ = bf16[272,1536]{1,0:T(8,128)(2,1)} slice(bf16[528,1536]{1,0:T(8,128)(2,1)} %collective-permute-done.12.refs_6_), slice={[256:528], [0:1536]} | slice | bytes 1671168 | tf_op jit(solution)/shard_map/slice | solution.py:533
  42.3 3.8 %collective-permute-start.15 = (bf16[272,1536]{1,0:T(8,128)(2,1)}, bf16[272,1536]{1,0:T(8,128)(2,1)}, u32[]{:S(2)}, u32[]{:S(2)}) collective-permute-start(bf16[272,1536]{1,0:T(8,128)(2,1)} %shard_map.104), channel_id=1, source_target_pairs={{0,6},{2,0},{4,2},{6,4},{1,7},{3,1},{5,3},{7,5},{8,14},{10,8},{12,... | collective-permute-start | bytes 2506760 | tf_op jit(solution)/shard_map/ppermute | solution.py:480
  46.1 2.2 %slice.72.refs_0_ = bf16[256,1536]{1,0:T(8,128)(2,1)} slice(bf16[528,1536]{1,0:T(8,128)(2,1)} %collective-permute-done.10.refs_4_), slice={[0:256], [0:1536]} | slice | bytes 1572864 | tf_op jit(solution)/shard_map/slice | solution.py:532
  48.4 3.0 %copy-done = bf16[3,1536,768]{2,1,0:T(8,128)(2,1)S(1)} copy-done((bf16[3,1536,768]{2,1,0:T(8,128)(2,1)S(1)}, bf16[3,1536,768]{2,1,0:T(8,128)(2,1)}, u32[]{:S(2)}) %copy-start) | copy-done | bytes 7077912
  52.7 3.9 %shard_map.101 = (f32[256,768]{1,0:T(8,128)S(1)}, bf16[128,1536]{1,0:T(8,128)(2,1)S(1)}, bf16[128,1536]{1,0:T(8,128)(2,1)S(1)}, f32[8,128]{1,0:T(8,128)S(1)}) custom-call(s32[1]{0:T(128)} %bitcast.6.core_ref, bf16[384,1536]{1,0:T(8,128)(2,1)S(1)} %copy-done.14, bf16[256,1536]{1,0:T(8,128)(2,1)S(1)} %bitcast.53, bf16[3,1536,768]{2,1,0:T(8,128)(2,1)S(1)} %copy-done, ...), custom_call_target="tpu_custom_call" | custom-call | tf_op jit(solution)/shard_map/pallas_call | solution.py:249
  59.5 4.2 %collective-permute-done.15.refs_9_ = bf16[272,1536]{1,0:T(8,128)(2,1)} collective-permute-done((bf16[272,1536]{1,0:T(8,128)(2,1)}, bf16[272,1536]{1,0:T(8,128)(2,1)}, u32[]{:S(2)}, u32[]{:S(2)}) %collective-permute-start.15) | collective-permute-done | bytes 835616 | tf_op jit(solution)/shard_map/ppermute | solution.py:480
  63.7 2.1 %copy.22.refs_0_ = bf16[272,1536]{1,0:T(8,128)(2,1)} copy(bf16[272,1536]{1,0:T(8,128)(2,1)} %collective-permute-done.15.refs_9_) | data formatting | bytes 1671168
  77.1 2.4 %shard_map.112 = (bf16[24,128,128]{2,1,0:T(8,128)(2,1)S(1)}, f32[8,128]{1,0:T(8,128)}) custom-call(s32[24]{0:T(128)S(1)} %get-tuple-element.93.refs_0_, bf16[128,128,128]{2,1,0:T(8,128)(2,1)} %all-to-all-done.refs_1_), custom_call_target="tpu_custom_call" | custom-call | tf_op jit(solution)/shard_map/pallas_call | solution.py:160
  80.1 2.4 %shard_map.113 = (bf16[24,128,128]{2,1,0:T(8,128)(2,1)S(1)}, f32[8,128]{1,0:T(8,128)}) custom-call(s32[24]{0:T(128)S(1)} %get-tuple-element.92.refs_0_, bf16[128,128,128]{2,1,0:T(8,128)(2,1)} %all-to-all-done.refs_1_), custom_call_target="tpu_custom_call" | custom-call | tf_op jit(solution)/shard_map/pallas_call | solution.py:160
  82.5 4.0 %collective-permute-start.19 = (bf16[24,128,128]{2,1,0:T(8,128)(2,1)S(1)}, bf16[24,128,128]{2,1,0:T(8,128)(2,1)S(1)}, u32[]{:S(2)}, u32[]{:S(2)}) collective-permute-start(bf16[24,128,128]{2,1,0:T(8,128)(2,1)S(1)} %get-tuple-element.71), channel_id=1, source_target_pairs={{0,4},{2,6},{4,0},{6,2},{1,5},{3,7},{5,1},{7,3},{8,12},{10,14},{12... | collective-permute-start | bytes 2359304 | tf_op jit(solution)/shard_map/ppermute | solution.py:480
  86.5 2.4 %shard_map.114 = (bf16[24,128,128]{2,1,0:T(8,128)(2,1)S(1)}, f32[8,128]{1,0:T(8,128)}) custom-call(s32[24]{0:T(128)S(1)} %get-tuple-element.91.refs_0_, bf16[128,128,128]{2,1,0:T(8,128)(2,1)} %all-to-all-done.refs_1_), custom_call_target="tpu_custom_call" | custom-call | tf_op jit(solution)/shard_map/pallas_call | solution.py:160
  89.1 3.8 %shard_map.110 = (bf16[64,128,128]{2,1,0:T(8,128)(2,1)S(1)}, f32[8,128]{1,0:T(8,128)}) custom-call(s32[64]{0:T(128)S(1)} %slice_bitcast_fusion.11.refs_0_, bf16[128,128,128]{2,1,0:T(8,128)(2,1)} %all-to-all-done.refs_1_), custom_call_target="tpu_custom_call" | custom-call | tf_op jit(solution)/shard_map/pallas_call | solution.py:160
  93.0 12.2 %shard_map.111 = (f32[256,4096]{1,0:T(8,128)S(1)}, f32[256,4096]{1,0:T(8,128)S(1)}, bf16[4096,1536]{1,0:T(8,128)(2,1)S(1)}) custom-call(bf16[128,1536]{1,0:T(8,128)(2,1)S(1)} %copy-done.22, bf16[128,1536]{1,0:T(8,128)(2,1)} %collective-permute-done.8.refs_2_.refs_1_, bf16[528,1536]{1,0:T(8,128)(2,1)S(1)} %copy-done.2, ...), custom_call_target="tpu_custom_call" | custom-call | tf_op jit(solution)/shard_map/pallas_call | solution.py:300
  105.2 13.2 %collective-permute-done.19.refs_5_ = bf16[24,128,128]{2,1,0:T(8,128)(2,1)S(1)} collective-permute-done((bf16[24,128,128]{2,1,0:T(8,128)(2,1)S(1)}, bf16[24,128,128]{2,1,0:T(8,128)(2,1)S(1)}, u32[]{:S(2)}, u32[]{:S(2)}) %collective-permute-start.19) | collective-permute-done | bytes 786464 | tf_op jit(solution)/shard_map/ppermute | solution.py:480
  126.8 5.3 %collective-permute-start.22 = (bf16[64,768]{1,0:T(8,128)(2,1)S(1)}, bf16[64,768]{1,0:T(8,128)(2,1)S(1)}, u32[]{:S(2)}, u32[]{:S(2)}) collective-permute-start(bf16[64,768]{1,0:T(8,128)(2,1)S(1)} %get-tuple-element.77), channel_id=1, source_target_pairs={{0,8},{8,16},{16,24},{24,32},{32,40},{40,48},{48,56},{56,64},{64,7... | collective-permute-start | bytes 294920 | tf_op jit(solution)/shard_map/ppermute | solution.py:25
  134.1 2.3 %shard_map.117.act_ref = f32[256,1536]{1,0:T(8,128)S(1)} custom-call(bf16[256,768]{1,0:T(8,128)(2,1)S(1)} %get-tuple-element.79.pre_ref, bf16[3,1536,768]{2,1,0:T(8,128)(2,1)S(1)} %bitcast.51), custom_call_target="tpu_custom_call" | custom-call | tf_op jit(solution)/shard_map/pallas_call | solution.py:410
  136.4 4.5 %collective-permute-done.23.after_ref = bf16[64,768]{1,0:T(8,128)(2,1)S(1)} collective-permute-done((bf16[64,768]{1,0:T(8,128)(2,1)S(1)}, bf16[64,768]{1,0:T(8,128)(2,1)S(1)}, u32[]{:S(2)}, u32[]{:S(2)}) %collective-permute-start.23) | collective-permute-done | bytes 98336 | tf_op jit(solution)/shard_map/ppermute | solution.py:25
  140.8 3.0 %shard_map.118 = f32[256,1536]{1,0:T(8,128)} custom-call(bf16[64,768]{1,0:T(8,128)(2,1)S(1)} %collective-permute-done.22.before_ref, bf16[64,768]{1,0:T(8,128)(2,1)S(1)} %collective-permute-done.23.after_ref, f32[256,1536]{1,0:T(8,128)S(1)} %shard_map.117.act_ref, bf16[3,1536,768]{2,1,0:T(8,128)(2,1)S(1)} %bitcast.51, bf16[3,1536,768]{2,1,0:T(8,128)(2,1)S(1)} %bitcast.51, ...), custom_call_target="tpu_custom_call" | custom-call | tf_op jit(solution)/shard_map/pallas_call | solution.py:444
  (155 shorter events, 38.2 us)
Async XLA Ops:
  2.2 11.3 %copy-start.34 = (s32[512]{0:T(512)S(1)}, s32[512]{0:T(512)}, u32[]{:S(2)}) copy-start(s32[512]{0:T(512)} %param.22) | copy-start | bytes 6148
  2.6 11.2 %copy-start.1 = (bf16[528,1536]{1,0:T(8,128)(2,1)}, bf16[528,1536]{1,0:T(8,128)(2,1)S(1)}, u32[]{:S(2)}) copy-start(bf16[528,1536]{1,0:T(8,128)(2,1)S(1)} %shard_map.102.rest_0_.refs_2_) | copy-start | bytes 4866052
  2.6 37.5 %collective-permute-start.12 = (bf16[528,1536]{1,0:T(8,128)(2,1)S(1)}, bf16[528,1536]{1,0:T(8,128)(2,1)}, u32[]{:S(2)}, u32[]{:S(2)}) collective-permute-start(bf16[528,1536]{1,0:T(8,128)(2,1)S(1)} %shard_map.102.rest_0_.refs_2_), channel_id=1, source_target_pairs={{0,6},{2,0},{4,2},{6,4},{1,7},{3,1},{5,3},{7,5},{8,14},{10,8},{12,... | collective-permute-start | bytes 4866056 | tf_op jit(solution)/shard_map/ppermute | solution.py:480
  5.5 40.7 %collective-permute-start.10 = (bf16[528,1536]{1,0:T(8,128)(2,1)S(1)}, bf16[528,1536]{1,0:T(8,128)(2,1)}, u32[]{:S(2)}, u32[]{:S(2)}) collective-permute-start(bf16[528,1536]{1,0:T(8,128)(2,1)S(1)} %shard_map.102.rest_0_.refs_2_), channel_id=1, source_target_pairs={{0,2},{2,4},{4,6},{6,0},{1,3},{3,5},{5,7},{7,1},{8,10},{10,12},{12... | collective-permute-start | bytes 4866056 | tf_op jit(solution)/shard_map/ppermute | solution.py:480
  5.5 12.4 %collective-permute-start.7 = (bf16[64,1536]{1,0:T(8,128)(2,1)S(1)}, bf16[64,1536]{1,0:T(8,128)(2,1)S(1)}, u32[]{:S(2)}, u32[]{:S(2)}) collective-permute-start(bf16[64,1536]{1,0:T(8,128)(2,1)S(1)} %get-tuple-element.89), channel_id=1, source_target_pairs={{8,0},{16,8},{24,16},{32,24},{40,32},{48,40},{56,48},{64,56},{72,6... | collective-permute-start | bytes 589832 | tf_op jit(solution)/shard_map/ppermute | solution.py:25
  8.2 9.8 %collective-permute-start.6 = (bf16[64,1536]{1,0:T(8,128)(2,1)S(1)}, bf16[64,1536]{1,0:T(8,128)(2,1)S(1)}, u32[]{:S(2)}, u32[]{:S(2)}) collective-permute-start(bf16[64,1536]{1,0:T(8,128)(2,1)S(1)} %get-tuple-element.90), channel_id=1, source_target_pairs={{0,8},{8,16},{16,24},{24,32},{32,40},{40,48},{48,56},{56,64},{64,7... | collective-permute-start | bytes 589832 | tf_op jit(solution)/shard_map/ppermute | solution.py:25
  19.4 15.5 %copy-start.18 = (bf16[64,1536]{1,0:T(8,128)(2,1)S(1)}, bf16[64,1536]{1,0:T(8,128)(2,1)}, u32[]{:S(2)}) copy-start(bf16[64,1536]{1,0:T(8,128)(2,1)} %copy-done.17) | copy-start | bytes 589828
  19.4 15.5 %copy-start.20 = (bf16[64,1536]{1,0:T(8,128)(2,1)S(1)}, bf16[64,1536]{1,0:T(8,128)(2,1)}, u32[]{:S(2)}) copy-start(bf16[64,1536]{1,0:T(8,128)(2,1)} %copy-done.19) | copy-start | bytes 589828
  19.4 56.0 %all-to-all-start = ((bf16[128,128,128]{2,1,0:T(8,128)(2,1)}), bf16[128,128,128]{2,1,0:T(8,128)(2,1)}, u32[]{:S(2)}, u32[]{:S(2)}) async-start(bf16[128,128,128]{2,1,0:T(8,128)(2,1)} %bitcast.55), calls=%async_computation | async-start | bytes 8388608 | tf_op jit(solution)/shard_map/all_to_all | solution.py:485
  42.3 21.4 %collective-permute-start.15 = (bf16[272,1536]{1,0:T(8,128)(2,1)}, bf16[272,1536]{1,0:T(8,128)(2,1)}, u32[]{:S(2)}, u32[]{:S(2)}) collective-permute-start(bf16[272,1536]{1,0:T(8,128)(2,1)} %shard_map.104), channel_id=1, source_target_pairs={{0,6},{2,0},{4,2},{6,4},{1,7},{3,1},{5,3},{7,5},{8,14},{10,8},{12,... | collective-permute-start | bytes 2506760 | tf_op jit(solution)/shard_map/ppermute | solution.py:480
  48.4 19.9 %collective-permute-start.14 = (bf16[256,1536]{1,0:T(8,128)(2,1)}, bf16[256,1536]{1,0:T(8,128)(2,1)}, u32[]{:S(2)}, u32[]{:S(2)}) collective-permute-start(bf16[256,1536]{1,0:T(8,128)(2,1)} %shard_map.103), channel_id=1, source_target_pairs={{0,2},{2,4},{4,6},{6,0},{1,3},{3,5},{5,7},{7,1},{8,10},{10,12},{12... | collective-permute-start | bytes 2359304 | tf_op jit(solution)/shard_map/ppermute | solution.py:480
  65.8 7.7 %collective-permute-start.17 = (bf16[272,1536]{1,0:T(8,128)(2,1)}, bf16[272,1536]{1,0:T(8,128)(2,1)}, u32[]{:S(2)}, u32[]{:S(2)}) collective-permute-start(bf16[272,1536]{1,0:T(8,128)(2,1)} %shard_map.106), channel_id=1, source_target_pairs={{0,1},{1,0},{2,3},{3,2},{4,5},{5,4},{6,7},{7,6},{8,9},{9,8},{10,11... | collective-permute-start | bytes 2506760 | tf_op jit(solution)/shard_map/ppermute | solution.py:29
  65.8 23.1 %collective-permute-start.9 = (bf16[528,1536]{1,0:T(8,128)(2,1)S(1)}, bf16[528,1536]{1,0:T(8,128)(2,1)S(1)}, u32[]{:S(2)}, u32[]{:S(2)}) collective-permute-start(bf16[528,1536]{1,0:T(8,128)(2,1)S(1)} %copy-done.2), channel_id=1, source_target_pairs={{0,1},{1,0},{2,3},{3,2},{4,5},{5,4},{6,7},{7,6},{8,9},{9,8},{10,11... | collective-permute-start | bytes 4866056 | tf_op jit(solution)/shard_map/ppermute | solution.py:29
  70.4 3.2 %collective-permute-start.16 = (bf16[256,1536]{1,0:T(8,128)(2,1)}, bf16[256,1536]{1,0:T(8,128)(2,1)}, u32[]{:S(2)}, u32[]{:S(2)}) collective-permute-start(bf16[256,1536]{1,0:T(8,128)(2,1)} %shard_map.105), channel_id=1, source_target_pairs={{0,1},{1,0},{2,3},{3,2},{4,5},{5,4},{6,7},{7,6},{8,9},{9,8},{10,11... | collective-permute-start | bytes 2359304 | tf_op jit(solution)/shard_map/ppermute | solution.py:29
  70.4 3.2 %collective-permute-start.8 = (bf16[128,1536]{1,0:T(8,128)(2,1)}, bf16[128,1536]{1,0:T(8,128)(2,1)}, u32[]{:S(2)}, u32[]{:S(2)}) collective-permute-start(bf16[128,1536]{1,0:T(8,128)(2,1)} %copy-done.26), channel_id=1, source_target_pairs={{0,1},{1,0},{2,3},{3,2},{4,5},{5,4},{6,7},{7,6},{8,9},{9,8},{10,11... | collective-permute-start | bytes 1179656 | tf_op jit(solution)/shard_map/ppermute | solution.py:29
  71.9 21.1 %collective-permute-start.13 = (bf16[528,1536]{1,0:T(8,128)(2,1)}, bf16[528,1536]{1,0:T(8,128)(2,1)}, u32[]{:S(2)}, u32[]{:S(2)}) collective-permute-start(bf16[528,1536]{1,0:T(8,128)(2,1)} %collective-permute-done.12.refs_6_), channel_id=1, source_target_pairs={{0,1},{1,0},{2,3},{3,2},{4,5},{5,4},{6,7},{7,6},{8,9},{9,8},{10,11... | collective-permute-start | bytes 4866056 | tf_op jit(solution)/shard_map/ppermute | solution.py:29
  75.4 17.6 %collective-permute-start.11 = (bf16[528,1536]{1,0:T(8,128)(2,1)}, bf16[528,1536]{1,0:T(8,128)(2,1)S(1)}, u32[]{:S(2)}, u32[]{:S(2)}) collective-permute-start(bf16[528,1536]{1,0:T(8,128)(2,1)} %collective-permute-done.10.refs_4_), channel_id=1, source_target_pairs={{0,1},{1,0},{2,3},{3,2},{4,5},{5,4},{6,7},{7,6},{8,9},{9,8},{10,11... | collective-permute-start | bytes 4866056 | tf_op jit(solution)/shard_map/ppermute | solution.py:29
  79.5 25.7 %collective-permute-start.18 = (bf16[24,128,128]{2,1,0:T(8,128)(2,1)S(1)}, bf16[24,128,128]{2,1,0:T(8,128)(2,1)S(1)}, u32[]{:S(2)}, u32[]{:S(2)}) collective-permute-start(bf16[24,128,128]{2,1,0:T(8,128)(2,1)S(1)} %get-tuple-element.70), channel_id=1, source_target_pairs={{0,2},{2,4},{4,6},{6,0},{1,3},{3,5},{5,7},{7,1},{8,10},{10,12},{12... | collective-permute-start | bytes 2359304 | tf_op jit(solution)/shard_map/ppermute | solution.py:480
  82.5 35.8 %collective-permute-start.19 = (bf16[24,128,128]{2,1,0:T(8,128)(2,1)S(1)}, bf16[24,128,128]{2,1,0:T(8,128)(2,1)S(1)}, u32[]{:S(2)}, u32[]{:S(2)}) collective-permute-start(bf16[24,128,128]{2,1,0:T(8,128)(2,1)S(1)} %get-tuple-element.71), channel_id=1, source_target_pairs={{0,4},{2,6},{4,0},{6,2},{1,5},{3,7},{5,1},{7,3},{8,12},{10,14},{12... | collective-permute-start | bytes 2359304 | tf_op jit(solution)/shard_map/ppermute | solution.py:480
  88.9 31.2 %collective-permute-start.20 = (bf16[24,128,128]{2,1,0:T(8,128)(2,1)S(1)}, bf16[24,128,128]{2,1,0:T(8,128)(2,1)S(1)}, u32[]{:S(2)}, u32[]{:S(2)}) collective-permute-start(bf16[24,128,128]{2,1,0:T(8,128)(2,1)S(1)} %get-tuple-element.72), channel_id=1, source_target_pairs={{0,6},{2,0},{4,2},{6,4},{1,7},{3,1},{5,3},{7,5},{8,14},{10,8},{12,... | collective-permute-start | bytes 2359304 | tf_op jit(solution)/shard_map/ppermute | solution.py:480
  93.0 27.1 %copy-start.24 = (s32[65]{0:T(128)S(1)}, s32[65]{0:T(128)}, u32[]{:S(2)}) copy-start(s32[65]{0:T(128)} %pad_add_fusion.refs_1_.refs_0_) | copy-start | bytes 784
  123.5 2.4 %collective-permute-start.21 = (f32[128,1536]{1,0:T(8,128)S(1)}, f32[128,1536]{1,0:T(8,128)S(1)}, u32[]{:S(2)}, u32[]{:S(2)}) collective-permute-start(f32[128,1536]{1,0:T(8,128)S(1)} %fusion.18), channel_id=1, source_target_pairs={{0,1},{1,0},{2,3},{3,2},{4,5},{5,4},{6,7},{7,6},{8,9},{9,8},{10,11... | collective-permute-start | bytes 2359304 | tf_op jit(solution)/shard_map/ppermute | solution.py:29
  126.8 9.6 %collective-permute-start.22 = (bf16[64,768]{1,0:T(8,128)(2,1)S(1)}, bf16[64,768]{1,0:T(8,128)(2,1)S(1)}, u32[]{:S(2)}, u32[]{:S(2)}) collective-permute-start(bf16[64,768]{1,0:T(8,128)(2,1)S(1)} %get-tuple-element.77), channel_id=1, source_target_pairs={{0,8},{8,16},{16,24},{24,32},{32,40},{40,48},{48,56},{56,64},{64,7... | collective-permute-start | bytes 294920 | tf_op jit(solution)/shard_map/ppermute | solution.py:25
  132.1 8.8 %collective-permute-start.23 = (bf16[64,768]{1,0:T(8,128)(2,1)S(1)}, bf16[64,768]{1,0:T(8,128)(2,1)S(1)}, u32[]{:S(2)}, u32[]{:S(2)}) collective-permute-start(bf16[64,768]{1,0:T(8,128)(2,1)S(1)} %get-tuple-element.78), channel_id=1, source_target_pairs={{8,0},{16,8},{24,16},{32,24},{40,32},{48,40},{56,48},{64,56},{72,6... | collective-permute-start | bytes 294920 | tf_op jit(solution)/shard_map/ppermute | solution.py:25
  (38 other events, 186.3 us)
